TPU v7x, 512 devices: a whole 4x8x8 slice. The times are simulated.
512 devices in a mesh: tm: 16 (over y, core), space: 32 (over x, z).
Axes of the slice: x: 4, y: 8, z: 8, core: 2. Of those that a mesh axis runs over, the one named last changes fastest.
Arguments:
- latent: bfloat16 [16, 2048, 2560], P('tm', 'space'), may hold values from -44 to 44
- past_cache: bfloat16 [2, 256, 81920], P(None, 'tm', 'space'), may hold values from -5 to 5
- neighbour_mask: int32 [16, 32, 4], P('tm', 'space'), may hold values 0 or 1
- gains: float32 [2, 2560], replicated, may hold values from 0.45 to 1.25
- step_sizes: float32 [2], replicated, may hold values from 0.3 to 0.8
Outputs:
- denoised: bfloat16 [16, 2048, 2560], P('tm', 'space')
- velocity: bfloat16 [16, 2048, 2560], P('tm', 'space')
All inputs are finite; a program needn't handle non-finite values. No bound on the sum of `neighbour_mask` on one device may be relied on, other than what follows from the above.
Results may differ from a plain program's by a relative error of at most 0.0069.
The roundings to bfloat16 on the way count: a program that leaves them out, or rounds other values in their place, can miss the bound.
Values may be sent and summed in bfloat16 or wider, within the bound.
A program may use at most 64 MiB of HBM per device.

v0:
```python
import jax
import jax.numpy as jnp
from jax import lax
from jax.sharding import PartitionSpec as P

HD = 128
HEADS = 20
STEPS = 2
OFFSETS = 4


epsilon = 1e-06


def passed_along(block, axis, distance):
    devices = range(lax.axis_size(axis))
    route = [(i - distance, i) for i in devices if i - distance in devices]
    return lax.ppermute(block, axis, route)


def normed(values):
    values = values.astype(jnp.float32)
    return values * lax.rsqrt(jnp.mean(values * values, axis=-1, keepdims=True) + epsilon)


def head_scores(query, keys):
    rows = query.shape[0]
    q_heads = query.reshape(rows, HEADS, HD)
    k_heads = keys.reshape(keys.shape[0], HEADS, HD)
    scores = jnp.einsum("thd,nhd->htn", q_heads, k_heads, preferred_element_type=jnp.float32)
    return scores / jnp.sqrt(jnp.float32(HD))


def head_mix(weights, values):
    v_heads = values.reshape(values.shape[0], HEADS, HD)
    return jnp.einsum(
        "htn,nhd->htd", weights.astype(jnp.bfloat16), v_heads, preferred_element_type=jnp.float32
    )


def start_state(query, keys, values):
    scores = head_scores(query, keys)
    peak = jnp.max(scores, axis=-1)
    expo = jnp.exp(scores - peak[..., None])
    return (peak, jnp.sum(expo, axis=-1), head_mix(expo, values))


def attend(state, query, keys, values, usable=None):
    peak, total, accum = state
    scores = head_scores(query, keys)
    if usable is not None:
        scores = jnp.where(usable, scores, jnp.float32(-1e30))
    new_peak = jnp.maximum(peak, jnp.max(scores, axis=-1))
    factor = jnp.exp(peak - new_peak)
    expo = jnp.exp(scores - new_peak[..., None])
    total = total * factor + jnp.sum(expo, axis=-1)
    accum = accum * factor[..., None] + head_mix(expo, values)
    return (new_peak, total, accum)


def per_device(latent, past_cache, neighbour_mask, gains, step_sizes):
    offsets = (-2, -1, 1, 2)
    current = latent[0]
    rows = current.shape[0]
    width = current.shape[1]
    column = lax.axis_index("space")
    count = lax.axis_size("space")
    usables = []
    for slot in range(OFFSETS):
        offset = offsets[slot]
        usables.append(
            (neighbour_mask[0, 0, slot] > 0) & (column + offset >= 0) & (column + offset < count)
        )
    step_velocity = jnp.zeros((rows, width), jnp.float32)
    for section in range(STEPS):
        normal = normed(current)
        query = (normal * gains[0]).astype(jnp.bfloat16)
        key = (normal * gains[1]).astype(jnp.bfloat16)
        state = start_state(query, key, current)
        piece = lax.all_gather(past_cache, "tm", axis=1, tiled=True)
        state = attend(state, query, piece[0], piece[1])
        for slot in range(OFFSETS):
            offset = offsets[slot]
            arrived = passed_along(jnp.stack((key, current)), "space", -offset)
            other_keys = arrived[0]
            other_values = arrived[1]
            state = attend(state, query, other_keys, other_values, usables[slot])
        peak, total, accum = state
        attended = (accum / total[..., None]).transpose(1, 0, 2).reshape(rows, width)
        step_velocity = normed(attended)
        current = (current.astype(jnp.float32) + step_sizes[section] * step_velocity).astype(
            jnp.bfloat16
        )
    return (current[None], step_velocity.astype(jnp.bfloat16)[None])


def solution(mesh):
    in_specs = (P("tm", "space", None), P(None, "tm", "space"), P("tm", "space", None), P(), P())
    out_specs = (P("tm", "space", None), P("tm", "space", None))
    return jax.shard_map(
        per_device, mesh=mesh, in_specs=in_specs, out_specs=out_specs, check_vma=False
    )
```

profile of v0, /device:TPU:6, one launch (start us, length us, event | category | flops | bytes accessed | tf_op | source)
XLA Modules:
  0.0 200.8 jit_solution(8253808544198000110)
XLA Ops:
  7.2 1.8 copy.56
  12.3 11.2 %collective-permute-start.2 = (bf16[2,64,2560]{2,1,0:T(8,128)(2,1)S(1)}, bf16[2,64,2560]{2,1,0:T(8,128)(2,1)}, u32[]{:S(2)}, u32[]{:S(2)}) collective-permute-start(bf16[2,64,2560]{2,1,0:T(8,128)(2,1)S(1)} %pad_maximum_fusion), channel_id=1, source_target_pairs={{1,0},{2,1},{3,2},{4,3},{5,4},{6,5},{7,6},{8,7},{9,8},{10,9},{11,1... | collective-permute-start | bytes 1966088 | tf_op jit(solution)/shard_map/ppermute | solution.py:18
  23.5 2.5 %collective-permute-start.3 = (bf16[2,64,2560]{2,1,0:T(8,128)(2,1)S(1)}, bf16[2,64,2560]{2,1,0:T(8,128)(2,1)}, u32[]{:S(2)}, u32[]{:S(2)}) collective-permute-start(bf16[2,64,2560]{2,1,0:T(8,128)(2,1)S(1)} %pad_maximum_fusion), channel_id=1, source_target_pairs={{2,0},{3,1},{4,2},{5,3},{6,4},{7,5},{8,6},{9,7},{10,8},{11,9},{12,... | collective-permute-start | bytes 1966088 | tf_op jit(solution)/shard_map/ppermute | solution.py:18
  26.0 3.4 %collective-permute-start.1 = (bf16[2,64,2560]{2,1,0:T(8,128)(2,1)S(1)}, bf16[2,64,2560]{2,1,0:T(8,128)(2,1)}, u32[]{:S(2)}, u32[]{:S(2)}) collective-permute-start(bf16[2,64,2560]{2,1,0:T(8,128)(2,1)S(1)} %pad_maximum_fusion), channel_id=1, source_target_pairs={{0,1},{1,2},{2,3},{3,4},{4,5},{5,6},{6,7},{7,8},{8,9},{9,10},{10,1... | collective-permute-start | bytes 1966088 | tf_op jit(solution)/shard_map/ppermute | solution.py:18
  29.4 2.8 %collective-permute-start = (bf16[2,64,2560]{2,1,0:T(8,128)(2,1)S(1)}, bf16[2,64,2560]{2,1,0:T(8,128)(2,1)S(1)}, u32[]{:S(2)}, u32[]{:S(2)}) collective-permute-start(bf16[2,64,2560]{2,1,0:T(8,128)(2,1)S(1)} %pad_maximum_fusion), channel_id=1, source_target_pairs={{0,2},{1,3},{2,4},{3,5},{4,6},{5,7},{6,8},{7,9},{8,10},{9,11},{10,... | collective-permute-start | bytes 1966088 | tf_op jit(solution)/shard_map/ppermute | solution.py:18
  36.9 15.8 %collective-permute-done.2 = bf16[2,64,2560]{2,1,0:T(8,128)(2,1)} collective-permute-done((bf16[2,64,2560]{2,1,0:T(8,128)(2,1)S(1)}, bf16[2,64,2560]{2,1,0:T(8,128)(2,1)}, u32[]{:S(2)}, u32[]{:S(2)}) %collective-permute-start.2) | collective-permute-done | bytes 655392 | tf_op jit(solution)/shard_map/ppermute | solution.py:18
  54.8 10.8 %collective-permute-done.3 = bf16[2,64,2560]{2,1,0:T(8,128)(2,1)} collective-permute-done((bf16[2,64,2560]{2,1,0:T(8,128)(2,1)S(1)}, bf16[2,64,2560]{2,1,0:T(8,128)(2,1)}, u32[]{:S(2)}, u32[]{:S(2)}) %collective-permute-start.3) | collective-permute-done | bytes 655392 | tf_op jit(solution)/shard_map/ppermute | solution.py:18
  69.8 2.2 %collective-permute-done = bf16[2,64,2560]{2,1,0:T(8,128)(2,1)S(1)} collective-permute-done((bf16[2,64,2560]{2,1,0:T(8,128)(2,1)S(1)}, bf16[2,64,2560]{2,1,0:T(8,128)(2,1)S(1)}, u32[]{:S(2)}, u32[]{:S(2)}) %collective-permute-start) | collective-permute-done | bytes 655392 | tf_op jit(solution)/shard_map/ppermute | solution.py:18
  81.1 8.3 %fusion.142 = (bf16[1,256,2560]{2,0,1:T(2,128)(2,1)}, bf16[1,256,2560]{2,0,1:T(2,128)(2,1)}) fusion(bf16[2,256,2560]{2,0,1:T(2,128)(2,1)} %all-gather.2.cloned.1.call-done), kind=kLoop, calls=%fused_computation.207 | loop fusion | bytes 5242880 | tf_op jit(solution)/shard_map/slice | solution.py:81
  89.4 4.9 %copy.105 = bf16[1,256,2560]{1,2,0:T(8,128)(2,1)S(1)} copy(bf16[1,256,2560]{2,0,1:T(2,128)(2,1)} %get-tuple-element.28) | data formatting | bytes 2621440
  95.4 4.9 %copy.106 = bf16[1,256,2560]{1,2,0:T(8,128)(2,1)S(1)} copy(bf16[1,256,2560]{2,0,1:T(2,128)(2,1)} %get-tuple-element.29) | data formatting | bytes 2621440
  110.1 2.0 fusion.42
  113.0 5.4 %collective-permute-start.7 = (bf16[2,64,2560]{2,1,0:T(8,128)(2,1)}, bf16[2,64,2560]{2,1,0:T(8,128)(2,1)S(1)}, u32[]{:S(2)}, u32[]{:S(2)}) collective-permute-start(bf16[2,64,2560]{2,1,0:T(8,128)(2,1)} %pad_maximum_fusion.1), channel_id=1, source_target_pairs={{2,0},{3,1},{4,2},{5,3},{6,4},{7,5},{8,6},{9,7},{10,8},{11,9},{12,... | collective-permute-start | bytes 1966088 | tf_op jit(solution)/shard_map/ppermute | solution.py:18
  118.5 1.9 collective-permute-start.6
  120.4 3.9 %collective-permute-start.5 = (bf16[2,64,2560]{2,1,0:T(8,128)(2,1)}, bf16[2,64,2560]{2,1,0:T(8,128)(2,1)}, u32[]{:S(2)}, u32[]{:S(2)}) collective-permute-start(bf16[2,64,2560]{2,1,0:T(8,128)(2,1)} %pad_maximum_fusion.1), channel_id=1, source_target_pairs={{0,1},{1,2},{2,3},{3,4},{4,5},{5,6},{6,7},{7,8},{8,9},{9,10},{10,1... | collective-permute-start | bytes 1966088 | tf_op jit(solution)/shard_map/ppermute | solution.py:18
  124.3 3.1 %collective-permute-start.4 = (bf16[2,64,2560]{2,1,0:T(8,128)(2,1)}, bf16[2,64,2560]{2,1,0:T(8,128)(2,1)}, u32[]{:S(2)}, u32[]{:S(2)}) collective-permute-start(bf16[2,64,2560]{2,1,0:T(8,128)(2,1)} %pad_maximum_fusion.1), channel_id=1, source_target_pairs={{0,2},{1,3},{2,4},{3,5},{4,6},{5,7},{6,8},{7,9},{8,10},{9,11},{10,... | collective-permute-start | bytes 1966088 | tf_op jit(solution)/shard_map/ppermute | solution.py:18
  128.0 1.5 fusion.164
  129.5 18.4 %collective-permute-done.7 = bf16[2,64,2560]{2,1,0:T(8,128)(2,1)S(1)} collective-permute-done((bf16[2,64,2560]{2,1,0:T(8,128)(2,1)}, bf16[2,64,2560]{2,1,0:T(8,128)(2,1)S(1)}, u32[]{:S(2)}, u32[]{:S(2)}) %collective-permute-start.7) | collective-permute-done | bytes 655392 | tf_op jit(solution)/shard_map/ppermute | solution.py:18
  149.0 10.9 %collective-permute-done.6 = bf16[2,64,2560]{2,1,0:T(8,128)(2,1)} collective-permute-done((bf16[2,64,2560]{2,1,0:T(8,128)(2,1)}, bf16[2,64,2560]{2,1,0:T(8,128)(2,1)}, u32[]{:S(2)}, u32[]{:S(2)}) %collective-permute-start.6) | collective-permute-done | bytes 655392 | tf_op jit(solution)/shard_map/ppermute | solution.py:18
  159.9 1.9 fusion.144
  161.8 2.0 reshape_squeeze.71
  163.8 1.9 fusion.145
  165.8 1.9 reshape_squeeze.69
  167.7 2.3 %fusion.159 = (f32[20,64]{1,0:T(8,128)S(1)}, f32[20,64,64]{1,2,0:T(8,128)}) fusion(bf16[64,20,128]{2,1,0:T(8,128)(2,1)} %reshape_squeeze.73, bf16[64,20,128]{2,0,1:T(8,128)(2,1)S(1)} %copy-done.4, f32[64]{0:T(128)S(1)} %add_rsqrt_fusion.1, f32[20,128]{1,0:T(8,128)S(1)} %bitcast.272, pred[]{:T(512)S(6)} %and.32), kind=kOutput, calls=%fused_computation.224 | convolution fusion | flops 21871360 | bytes 998657 | tf_op jit(solution)/shard_map/thd,nhd->htn/dot_general | solution.py:30
  172.5 2.0 fusion.146
  174.4 1.9 reshape_squeeze.67
  176.3 2.2 %fusion.162 = (f32[20,64]{1,0:T(8,128)S(1)}, f32[20,64,64]{1,2,0:T(8,128)}) fusion(bf16[64,20,128]{2,1,0:T(8,128)(2,1)} %reshape_squeeze.67, bf16[64,20,128]{2,0,1:T(8,128)(2,1)S(1)} %copy-done.4, f32[64]{0:T(128)S(1)} %add_rsqrt_fusion.1, f32[20,128]{1,0:T(8,128)S(1)} %bitcast.275, pred[]{:T(512)S(6)} %and.26), kind=kOutput, calls=%fused_computation.227 | convolution fusion | flops 21871360 | bytes 998657 | tf_op jit(solution)/shard_map/thd,nhd->htn/dot_general | solution.py:30
  179.0 1.5 convolution_bitcast_fusion.10
  180.5 2.0 reshape_squeeze.68
  182.5 2.0 reshape_squeeze.70
  185.7 1.3 fusion.72
  192.3 1.6 multiply_convert_fusion.2
  (143 shorter events, 43.1 us)
Async XLA Ops:
  7.2 5.1 %copy-start.2 = (bf16[1,64,2560]{2,1,0:T(8,128)(2,1)S(1)}, bf16[1,64,2560]{2,1,0:T(8,128)(2,1)}, u32[]{:S(2)}) copy-start(bf16[1,64,2560]{2,1,0:T(8,128)(2,1)} %param.5) | copy-start | bytes 983044
  7.2 73.9 %all-gather.2.cloned.1.call-start = ((), (), s32[]{:S(2)}) async-start(), calls=%async_computation | async-start | bytes 2785280 | tf_op jit(solution)/shard_map/all_gather | solution.py:80
  11.1 21.4 %copy-start.33 = (s32[1,1,4]{2,1,0:T(1,128)S(1)}, s32[1,1,4]{2,1,0:T(1,128)}, u32[]{:S(2)}) copy-start(s32[1,1,4]{2,1,0:T(1,128)} %param.7) | copy-start | bytes 52
  11.1 24.6 %copy-start.34 = (f32[2]{0:T(128)S(1)}, f32[2]{0:T(128)}, u32[]{:S(2)}) copy-start(f32[2]{0:T(128)} %param.9) | copy-start | bytes 28
  12.3 40.4 %collective-permute-start.2 = (bf16[2,64,2560]{2,1,0:T(8,128)(2,1)S(1)}, bf16[2,64,2560]{2,1,0:T(8,128)(2,1)}, u32[]{:S(2)}, u32[]{:S(2)}) collective-permute-start(bf16[2,64,2560]{2,1,0:T(8,128)(2,1)S(1)} %pad_maximum_fusion), channel_id=1, source_target_pairs={{1,0},{2,1},{3,2},{4,3},{5,4},{6,5},{7,6},{8,7},{9,8},{10,9},{11,1... | collective-permute-start | bytes 1966088 | tf_op jit(solution)/shard_map/ppermute | solution.py:18
  23.5 42.1 %collective-permute-start.3 = (bf16[2,64,2560]{2,1,0:T(8,128)(2,1)S(1)}, bf16[2,64,2560]{2,1,0:T(8,128)(2,1)}, u32[]{:S(2)}, u32[]{:S(2)}) collective-permute-start(bf16[2,64,2560]{2,1,0:T(8,128)(2,1)S(1)} %pad_maximum_fusion), channel_id=1, source_target_pairs={{2,0},{3,1},{4,2},{5,3},{6,4},{7,5},{8,6},{9,7},{10,8},{11,9},{12,... | collective-permute-start | bytes 1966088 | tf_op jit(solution)/shard_map/ppermute | solution.py:18
  26.0 41.7 %collective-permute-start.1 = (bf16[2,64,2560]{2,1,0:T(8,128)(2,1)S(1)}, bf16[2,64,2560]{2,1,0:T(8,128)(2,1)}, u32[]{:S(2)}, u32[]{:S(2)}) collective-permute-start(bf16[2,64,2560]{2,1,0:T(8,128)(2,1)S(1)} %pad_maximum_fusion), channel_id=1, source_target_pairs={{0,1},{1,2},{2,3},{3,4},{4,5},{5,6},{6,7},{7,8},{8,9},{9,10},{10,1... | collective-permute-start | bytes 1966088 | tf_op jit(solution)/shard_map/ppermute | solution.py:18
  29.4 42.6 %collective-permute-start = (bf16[2,64,2560]{2,1,0:T(8,128)(2,1)S(1)}, bf16[2,64,2560]{2,1,0:T(8,128)(2,1)S(1)}, u32[]{:S(2)}, u32[]{:S(2)}) collective-permute-start(bf16[2,64,2560]{2,1,0:T(8,128)(2,1)S(1)} %pad_maximum_fusion), channel_id=1, source_target_pairs={{0,2},{1,3},{2,4},{3,5},{4,6},{5,7},{6,8},{7,9},{8,10},{9,11},{10,... | collective-permute-start | bytes 1966088 | tf_op jit(solution)/shard_map/ppermute | solution.py:18
  36.7 18.1 %copy-start.7 = (f32[20,64,64]{1,2,0:T(8,128)}, f32[20,64,64]{1,2,0:T(8,128)S(1)}, u32[]{:S(2)}) copy-start(f32[20,64,64]{1,2,0:T(8,128)S(1)} %get-tuple-element.63) | copy-start | bytes 983044
  72.2 3.9 %copy-start.28 = (bf16[64,20,128]{2,1,0:T(8,128)(2,1)S(1)}, bf16[64,20,128]{2,1,0:T(8,128)(2,1)}, u32[]{:S(2)}) copy-start(bf16[64,20,128]{2,1,0:T(8,128)(2,1)} %reshape_squeeze.63) | copy-start | bytes 983044
  75.1 2.2 %copy-start.29 = (bf16[64,20,128]{2,1,0:T(8,128)(2,1)S(1)}, bf16[64,20,128]{2,1,0:T(8,128)(2,1)}, u32[]{:S(2)}) copy-start(bf16[64,20,128]{2,1,0:T(8,128)(2,1)} %reshape_squeeze.65) | copy-start | bytes 983044
  77.4 1.2 copy-start.30
  100.8 1.3 copy-start.25
  101.4 1.2 copy-start.14
  101.5 1.4 copy-start.15
  109.1 18.3 %copy-start.3 = (bf16[64,20,128]{2,0,1:T(8,128)(2,1)}, bf16[64,20,128]{2,0,1:T(8,128)(2,1)S(1)}, u32[]{:S(2)}) copy-start(bf16[64,20,128]{2,0,1:T(8,128)(2,1)S(1)} %fusion.40) | copy-start | bytes 983044
  112.0 15.8 %copy-start.5 = (bf16[1,64,2560]{2,1,0:T(8,128)(2,1)}, bf16[1,64,2560]{2,1,0:T(8,128)(2,1)S(1)}, u32[]{:S(2)}) copy-start(bf16[1,64,2560]{2,1,0:T(8,128)(2,1)S(1)} %get-tuple-element.16) | copy-start | bytes 983044
  113.0 15.0 %copy-start.1 = (bf16[1,256,2560]{1,2,0:T(8,128)(2,1)S(1)}, bf16[1,256,2560]{1,2,0:T(8,128)(2,1)}, u32[]{:S(2)}) copy-start(bf16[1,256,2560]{1,2,0:T(8,128)(2,1)} %copy-done) | copy-start | bytes 3932164
  113.0 34.9 %collective-permute-start.7 = (bf16[2,64,2560]{2,1,0:T(8,128)(2,1)}, bf16[2,64,2560]{2,1,0:T(8,128)(2,1)S(1)}, u32[]{:S(2)}, u32[]{:S(2)}) collective-permute-start(bf16[2,64,2560]{2,1,0:T(8,128)(2,1)} %pad_maximum_fusion.1), channel_id=1, source_target_pairs={{2,0},{3,1},{4,2},{5,3},{6,4},{7,5},{8,6},{9,7},{10,8},{11,9},{12,... | collective-permute-start | bytes 1966088 | tf_op jit(solution)/shard_map/ppermute | solution.py:18
  118.5 41.4 %collective-permute-start.6 = (bf16[2,64,2560]{2,1,0:T(8,128)(2,1)}, bf16[2,64,2560]{2,1,0:T(8,128)(2,1)}, u32[]{:S(2)}, u32[]{:S(2)}) collective-permute-start(bf16[2,64,2560]{2,1,0:T(8,128)(2,1)} %pad_maximum_fusion.1), channel_id=1, source_target_pairs={{1,0},{2,1},{3,2},{4,3},{5,4},{6,5},{7,6},{8,7},{9,8},{10,9},{11,1... | collective-permute-start | bytes 1966088 | tf_op jit(solution)/shard_map/ppermute | solution.py:18
  120.4 43.4 %collective-permute-start.5 = (bf16[2,64,2560]{2,1,0:T(8,128)(2,1)}, bf16[2,64,2560]{2,1,0:T(8,128)(2,1)}, u32[]{:S(2)}, u32[]{:S(2)}) collective-permute-start(bf16[2,64,2560]{2,1,0:T(8,128)(2,1)} %pad_maximum_fusion.1), channel_id=1, source_target_pairs={{0,1},{1,2},{2,3},{3,4},{4,5},{5,6},{6,7},{7,8},{8,9},{9,10},{10,1... | collective-permute-start | bytes 1966088 | tf_op jit(solution)/shard_map/ppermute | solution.py:18
  124.3 48.1 %collective-permute-start.4 = (bf16[2,64,2560]{2,1,0:T(8,128)(2,1)}, bf16[2,64,2560]{2,1,0:T(8,128)(2,1)}, u32[]{:S(2)}, u32[]{:S(2)}) collective-permute-start(bf16[2,64,2560]{2,1,0:T(8,128)(2,1)} %pad_maximum_fusion.1), channel_id=1, source_target_pairs={{0,2},{1,3},{2,4},{3,5},{4,6},{5,7},{6,8},{7,9},{8,10},{9,11},{10,... | collective-permute-start | bytes 1966088 | tf_op jit(solution)/shard_map/ppermute | solution.py:18
  127.8 1.7 copy-start.9
  161.8 5.9 %copy-start.4 = (bf16[64,20,128]{2,0,1:T(8,128)(2,1)S(1)}, bf16[64,20,128]{2,0,1:T(8,128)(2,1)}, u32[]{:S(2)}) copy-start(bf16[64,20,128]{2,0,1:T(8,128)(2,1)} %copy-done.3) | copy-start | bytes 983044
  167.7 2.3 %copy-start.31 = (bf16[64,20,128]{2,1,0:T(8,128)(2,1)S(1)}, bf16[64,20,128]{2,1,0:T(8,128)(2,1)}, u32[]{:S(2)}) copy-start(bf16[64,20,128]{2,1,0:T(8,128)(2,1)} %reshape_squeeze.71) | copy-start | bytes 983044
  167.7 3.5 %copy-start.32 = (bf16[64,20,128]{2,1,0:T(8,128)(2,1)S(1)}, bf16[64,20,128]{2,1,0:T(8,128)(2,1)}, u32[]{:S(2)}) copy-start(bf16[64,20,128]{2,1,0:T(8,128)(2,1)} %reshape_squeeze.69) | copy-start | bytes 983044
  180.5 4.0 %copy-start.23 = (bf16[1,64,2560]{2,1,0:T(8,128)(2,1)S(1)}, bf16[1,64,2560]{2,1,0:T(8,128)(2,1)}, u32[]{:S(2)}) copy-start(bf16[1,64,2560]{2,1,0:T(8,128)(2,1)} %get-tuple-element.34) | copy-start | bytes 983044
  182.5 4.5 %copy-start.11 = (f32[20,64,64]{1,2,0:T(8,128)S(1)}, f32[20,64,64]{1,2,0:T(8,128)}, u32[]{:S(2)}) copy-start(f32[20,64,64]{1,2,0:T(8,128)} %get-tuple-element.71) | copy-start | bytes 983044
  184.5 2.7 %copy-start.13 = (f32[20,64,64]{1,2,0:T(8,128)S(1)}, f32[20,64,64]{1,2,0:T(8,128)}, u32[]{:S(2)}) copy-start(f32[20,64,64]{1,2,0:T(8,128)} %get-tuple-element.73) | copy-start | bytes 983044
  184.7 2.6 %copy-start.16 = (f32[20,64,64]{1,2,0:T(8,128)S(1)}, f32[20,64,64]{1,2,0:T(8,128)}, u32[]{:S(2)}) copy-start(f32[20,64,64]{1,2,0:T(8,128)} %get-tuple-element.75) | copy-start | bytes 983044
  185.7 1.8 copy-start.10
  185.7 1.8 copy-start.17
  (12 other events, 12.7 us)
Sparse Core Ops, SparseCore 0:
  10.7 47.1 all-gather.1
where the time goes:
time: 202 us; the launch traced here: 201 us
  waiting for transfers between devices  58.1 us (29%)
  local copies, waits for them, and re-layouts  57.4 us (28%)
  starting transfers between devices  34.3 us (17%)
  matrix products  21.5 us (11%)
  between operations  17.3 us (9%)
  other arithmetic  12.3 us (6%)
    ppermute x8, waiting for transfers between devices, passed_along(): return lax.ppermute(block, axis, route)  58.1 us
    ppermute x8, starting transfers between devices, passed_along(): return lax.ppermute(block, axis, route)  34.2 us
    unnamed x73, local copies, waits for them, and re-layouts  16.6 us
    dot_general x12, matrix products, head_scores(): jnp.einsum('thd,nhd->htn', q_heads, k_heads, preferred_element_type=jnp.f...  14.7 us
    another operation x8, local copies, waits for them, and re-layouts, head_scores(): k_heads = keys.reshape(keys.shape[0], HEADS, HD)  9.94 us
    slice x8, local copies, waits for them, and re-layouts, per_device(): other_values = arrived[1]  9.28 us
    another operation x8, local copies, waits for them, and re-layouts, head_mix(): v_heads = values.reshape(values.shape[0], HEADS, HD)  9 us
    slice x1, local copies, waits for them, and re-layouts, per_device(): state = attend(state, query, piece[0], piece[1])  8.3 us
  transfers between devices with their start and end apart: 9, of which 5 were waited for; matrix products, arithmetic and copies ran while one was open for 18% of the time, Pallas kernels for 0%

commit v1 on v0

v1 whole, which is shorter than its diff:
```python
import math

import jax
import jax.numpy as jnp
from jax import lax
from jax.experimental import pallas as pl
from jax.experimental.pallas import tpu as pltpu
from jax.sharding import PartitionSpec as P

HD = 128
HEADS = 20
HW = HD * HEADS
TOK = 64
STEPS = 2
SHARD = 16
GROUPS = 4
PER = HEADS // GROUPS
GW = PER * HD
BATCH = 20
EPS = 1e-6
SCORE_SCALE = math.log2(math.e) / math.sqrt(HD)
MASKED = -1e30
MESH = pl.DeviceIdType.MESH
F32 = jnp.float32
BF16 = jnp.bfloat16

STAGE = 128
NEAR, FAR = 3, 4
TILES = 3 * STAGE
ROWS = TILES + STEPS * 2 * STAGE
CHIP = TOK
RING = 14


def kernel(
    latent_hbm, cache_hbm, mask_hbm, gains_hbm, steps_hbm,
    denoised_ref, velocity_ref,
    mask_ref, gains_ref, steps_ref, buf, query, accum, peak, total, scale_own, scale_in, scale_col, bias, square,
    local_sem, ysend, ssend, yrecv, zsend, zrecv, rsend, rrecv,
):
    tm, space = lax.axis_index("tm"), lax.axis_index("space")
    n_tm, n_space = lax.axis_size("tm"), lax.axis_size("space")
    along_y = ((lax.rem(tm + 2, n_tm), space), (lax.rem(tm + n_tm - 2, n_tm), space))
    sibling = (tm + 1 - 2 * lax.rem(tm, 2), space)
    along_z = ((tm, lax.rem(space + 1, n_space)), (tm, lax.rem(space + n_space - 1, n_space)))
    has_low, has_high = space > 0, space < n_space - 1
    sends = ((has_high, has_low & has_high), (has_low, has_low & has_high))
    receives = ((has_low, space > 1), (has_high, space < n_space - 2))

    def remote(src, dst, send, recv, device):
        return pltpu.make_async_remote_copy(
            src_ref=src, dst_ref=dst, send_sem=send, recv_sem=recv, device_id=device, device_id_type=MESH
        )

    def half_cols(half):
        return pl.ds(pl.multiple_of(half * (HW // 2), HW // 2), HW // 2)

    def shard(which, index, half):
        rows = CHIP + SHARD * index + jnp.where(index >= 2, 2 * SHARD, 0)
        return buf.at[which, pl.ds(pl.multiple_of(rows, SHARD), SHARD), half_cols(half)]

    def slot(distance, direction):
        return 4 * distance - 2 + jnp.where(distance == 4, 0, 2 * direction)

    def ring_place(direction, number):
        which = lax.rem(number // 2 + direction, 2)
        return which, lax.rem(number, 2), number // 4 + 1

    def ring_copy(direction, number, own):
        which, half, distance = ring_place(direction, number)
        target = slot(distance, direction)
        if own:
            src = cache_hbm.at[which, :, half_cols(half)]
        else:
            src = shard(which, slot(distance - 1, direction), half)
        return remote(
            src, shard(which, target, half), ysend.at[direction, number], yrecv.at[which, target, half],
            along_y[direction],
        )

    def sib_copy(which, half, target, own=False):
        src = cache_hbm.at[which, :, half_cols(half)] if own else shard(which, target - 1, half)
        return remote(
            src, shard(which, target, half), ssend.at[which, target, half], yrecv.at[which, target, half], sibling
        )

    def ring_round(number):
        for direction in range(2):
            which, half, distance = ring_place(direction, number)
            ring_copy(direction, number, False).wait_recv()

            @pl.when(number + 4 < RING)
            def _():
                ring_copy(direction, number + 4, False).start()

            sib_copy(which, half, slot(distance, direction) + 1).start()

    def each_sibling(first, count, act):
        def body(i, _):
            act(sib_copy(lax.rem(i, 2), lax.rem(i // 2, 2), first + 2 * (i // 4)))
            return 0

        lax.fori_loop(0, 4 * count, body, 0)

    def columns(group):
        return pl.ds(pl.multiple_of(group * GW, GW), GW)

    def head_cols(head):
        return pl.ds(pl.multiple_of(head * HD, HD), HD)

    def tile_rows(phase, number):
        return pl.ds(pl.multiple_of(TILES + phase * 2 * STAGE + number * TOK, TOK), TOK)

    def tile_part(phase, number, cols):
        return buf.at[1, tile_rows(phase, number), cols]

    def tile_copy(phase, direction, hop, group):
        cols = columns(group)
        if hop == 1:
            src = tile_part(phase, direction, cols)
        elif isinstance(phase, int) and phase == 0:
            src = latent_hbm.at[0, :, cols]
        else:
            src = buf.at[1, pl.ds(0, TOK), cols]
        target = 2 * hop + direction
        return remote(
            src, tile_part(phase, target, cols), zsend.at[phase, direction, hop, group],
            zrecv.at[phase, target, group], along_z[direction],
        )

    def scale_copy(phase, direction, hop):
        src = scale_own.at[phase] if hop == 0 else scale_in.at[phase, direction]
        target = 2 * hop + direction
        return remote(
            src, scale_in.at[phase, target], rsend.at[phase, direction, hop], rrecv.at[phase, target], along_z[direction]
        )

    def start_tile(phase, hop, group):
        for direction in range(2):
            @pl.when(sends[direction][hop])
            def _():
                tile_copy(phase, direction, hop, group).start()

    def wait_tile(phase, hop, group):
        for direction in range(2):
            @pl.when(receives[direction][hop])
            def _():
                tile_copy(phase, direction, hop, group).wait_recv()

        if hop == 0:
            start_tile(phase, 1, group)

    diagonal = lax.broadcasted_iota(jnp.int32, (TOK, HD), 0) == lax.broadcasted_iota(jnp.int32, (TOK, HD), 1)

    def take_scales(phase, hop):
        for direction in range(2):
            target = 2 * hop + direction

            @pl.when(receives[direction][hop])
            def _():
                scale_copy(phase, direction, hop).wait_recv()

            if hop == 0:
                @pl.when(sends[direction][1])
                def _():
                    scale_copy(phase, direction, 1).start()

            row = jnp.broadcast_to(scale_in[phase, target, 0:1, :], (TOK, HD))
            col = jnp.sum(jnp.where(diagonal, row, 0.0), axis=1, keepdims=True)
            scale_col[pl.ds(target * TOK, TOK), :] = jnp.broadcast_to(col, (TOK, HD))

    def root_scale():
        mean = jnp.sum(square[...], axis=1, keepdims=True) * (1.0 / HW)
        return jnp.broadcast_to(lax.rsqrt(mean + EPS), (TOK, HD))

    def send_scale(phase, col):
        row = jnp.sum(jnp.where(diagonal, col, 0.0), axis=0, keepdims=True)
        scale_own[phase] = jnp.broadcast_to(row, (8, HD))
        for direction in range(2):
            @pl.when(sends[direction][0])
            def _():
                scale_copy(phase, direction, 0).start()

    def begin_heads(col):
        def body(group, _):
            heads = [group * PER + i for i in range(PER)]
            normals = [buf[1, pl.ds(0, TOK), head_cols(head)].astype(F32) * col for head in heads]
            for head, normal in zip(heads, normals):
                cols = head_cols(head)
                query[:, cols] = (normal * gains_ref[0:1, cols]).astype(BF16)
                buf[0, pl.ds(0, TOK), cols] = (normal * gains_ref[1:2, cols]).astype(BF16)
                peak[head] = jnp.full((TOK, HD), MASKED, F32)
                total[head] = jnp.zeros((TOK, HD), F32)
                accum[:, cols] = jnp.zeros((TOK, HD), F32)
            return 0

        lax.fori_loop(0, GROUPS, body, 0)

    def tile_keys(stage, phase, heads):
        scales = scale_col[pl.ds(pl.multiple_of((stage - NEAR) * STAGE, STAGE), STAGE), :]
        source = pl.ds(pl.multiple_of((stage + phase * 2) * STAGE, STAGE), STAGE)
        return [
            (buf[1, source, head_cols(head)].astype(F32) * scales * gains_ref[1:2, head_cols(head)]).astype(BF16)
            for head in heads
        ]

    def update(stage, phase, heads):
        cols = [head_cols(head) for head in heads]
        value_stage = stage + phase * 2 if stage >= NEAR else stage
        value_rows = pl.ds(pl.multiple_of(value_stage * STAGE, STAGE), STAGE)
        allowed = bias[stage, 0:1, :]
        if stage >= NEAR:
            keys = tile_keys(stage, phase, heads)
        else:
            keys = [buf[0, value_rows, c] for c in cols]
        queries = [query[:, c] for c in cols]
        old_peaks = [peak[head] for head in heads]
        scores = [
            lax.dot_general(q, k, (((1,), (1,)), ((), ())), preferred_element_type=F32) * SCORE_SCALE + allowed
            for q, k in zip(queries, keys)
        ]
        peaks = [
            jnp.maximum(old, jnp.broadcast_to(jnp.max(s, axis=1, keepdims=True), (TOK, HD)))
            for old, s in zip(old_peaks, scores)
        ]
        expos = [jnp.exp2(s - p) for s, p in zip(scores, peaks)]
        values = [buf[1, value_rows, c] for c in cols]
        mixed = [jnp.dot(e.astype(BF16), v, preferred_element_type=F32) for e, v in zip(expos, values)]
        factors = [jnp.exp2(old - new) for old, new in zip(old_peaks, peaks)]
        totals = [total[head] * f + e for head, f, e in zip(heads, factors, expos)]
        sums = [accum[:, c] * f + m for c, f, m in zip(cols, factors, mixed)]
        for i, head in enumerate(heads):
            peak[head] = peaks[i]
            total[head] = totals[i]
            accum[:, cols[i]] = sums[i]

    def finish(group, _):
        heads = [group * PER + i for i in range(PER)]
        squares = square[...]
        attended = [accum[:, head_cols(head)] / jnp.sum(total[head], axis=1, keepdims=True) for head in heads]
        for head, values in zip(heads, attended):
            accum[:, head_cols(head)] = values
            squares = squares + values * values
        square[...] = squares
        return 0

    loads = [
        pltpu.make_async_copy(latent_hbm.at[0], buf.at[1, pl.ds(0, TOK)], local_sem.at[0]),
        pltpu.make_async_copy(cache_hbm.at[0], buf.at[0, pl.ds(CHIP, SHARD)], local_sem.at[1]),
        pltpu.make_async_copy(cache_hbm.at[1], buf.at[1, pl.ds(CHIP, SHARD)], local_sem.at[2]),
        pltpu.make_async_copy(mask_hbm, mask_ref, local_sem.at[3]),
        pltpu.make_async_copy(gains_hbm, gains_ref, local_sem.at[4]),
        pltpu.make_async_copy(steps_hbm, steps_ref, local_sem.at[5]),
    ]
    for load in loads:
        load.start()
    barrier = pltpu.get_barrier_semaphore()
    for device in (*along_y, sibling):
        pl.semaphore_signal(barrier, inc=1, device_id=device, device_id_type=MESH)
    for direction in range(2):
        @pl.when(sends[direction][0])
        def _():
            pl.semaphore_signal(barrier, inc=1, device_id=along_z[direction], device_id_type=MESH)

    pl.semaphore_wait(barrier, 3 + lax.min(space, 1) + lax.min(n_space - 1 - space, 1))

    for number in range(2):
        for direction in range(2):
            ring_copy(direction, number, True).start()
    start_tile(0, 0, 0)
    for number in range(2, 4):
        for direction in range(2):
            ring_copy(direction, number, True).start()
    for which in range(2):
        for half in range(2):
            sib_copy(which, half, 1, True).start()

    for hop in range(2):
        for direction in range(2):
            @pl.when(jnp.logical_not(receives[direction][hop]))
            def _():
                for phase in range(STEPS):
                    buf[1, tile_rows(phase, 2 * hop + direction), :] = jnp.zeros((TOK, HW), BF16)
                    scale_in[phase, 2 * hop + direction] = jnp.zeros((8, HD), F32)

    for which in range(2):
        for stage in (0, 2):
            buf[which, pl.ds(stage * STAGE + 3 * STAGE // 4, STAGE // 4), :] = jnp.zeros((STAGE // 4, HW), BF16)

    for load in loads[3:]:
        load.wait()
    lane = lax.broadcasted_iota(jnp.int32, (8, HD), 1)
    for stage in (0, 2):
        bias[stage] = jnp.where(lane < 3 * STAGE // 4, 0.0, MASKED).astype(F32)
    bias[1] = jnp.zeros((8, HD), F32)
    for hop in range(2):
        low, high = (1, 2) if hop == 0 else (0, 3)
        low_ok = (mask_ref[0, 0, low] > 0) & (space - hop > 0)
        high_ok = (mask_ref[0, 0, high] > 0) & (space + hop + 1 < n_space)
        low_bias = jnp.where(low_ok, 0.0, MASKED).astype(F32)
        high_bias = jnp.where(high_ok, 0.0, MASKED).astype(F32)
        bias[NEAR + hop] = jnp.where(lane < TOK, low_bias, high_bias)

    loads[0].wait()
    square[...] = jnp.zeros((TOK, HD), F32)

    def add_squares(group, _):
        squares = square[...]
        for i in range(PER):
            values = buf[1, pl.ds(0, TOK), head_cols(group * PER + i)].astype(F32)
            squares = squares + values * values
        square[...] = squares
        return 0

    lax.fori_loop(0, GROUPS, add_squares, 0)
    col = root_scale()
    send_scale(0, col)
    for group in range(1, GROUPS):
        start_tile(0, 0, group)
    begin_heads(col)
    for load in loads[1:3]:
        load.wait()

    def phase_body(phase, _):
        first = phase == 0
        square[...] = jnp.zeros((TOK, HD), F32)

        def heads_of(part, count):
            return [part * count + i for i in range(count)]

        def arrive(hop, group, rounds=True):
            if rounds:
                @pl.when(first)
                def _():
                    ring_round(8 * hop + 2 * group)
                    ring_round(8 * hop + 2 * group + 1)

            wait_tile(phase, hop, group)

        @pl.when(first)
        def _():
            each_sibling(1, 1, lambda copy: copy.wait_recv())

        def stored(stage):
            def body(part, _):
                update(stage, phase, heads_of(part, BATCH))
                return 0

            lax.fori_loop(0, HEADS // BATCH, body, 0)

        stored(0)

        def near(part, _):
            arrive(0, 2 * part)

            @pl.when(part == 0)
            def _():
                take_scales(phase, 0)

            arrive(0, 2 * part + 1)
            update(NEAR, phase, heads_of(part, 2 * PER))
            return 0

        lax.fori_loop(0, GROUPS // 2, near, 0)

        @pl.when(first)
        def _():
            each_sibling(3, 4, lambda copy: copy.wait_recv())

        stored(1)
        arrive(1, 0)
        take_scales(phase, 1)
        arrive(1, 1)
        update(FAR, phase, heads_of(0, 2 * PER))
        arrive(1, 2)
        update(FAR, phase, heads_of(2, PER))

        @pl.when(first)
        def _():
            each_sibling(11, 3, lambda copy: copy.wait_recv())

        stored(2)
        lax.fori_loop(0, 3, finish, 0)
        arrive(1, 3, rounds=False)
        update(FAR, phase, heads_of(3, PER))
        finish(3, 0)

        @pl.when(first)
        def _():
            col = root_scale()
            step_size = steps_ref[0]
            square[...] = jnp.zeros((TOK, HD), F32)

            def move(group, _):
                squares = square[...]
                cols = [head_cols(group * PER + i) for i in range(PER)]
                moved = [
                    (buf[1, pl.ds(0, TOK), c].astype(F32) + step_size * (accum[:, c] * col)).astype(BF16)
                    for c in cols
                ]
                for c, values in zip(cols, moved):
                    buf[1, pl.ds(0, TOK), c] = values
                    wide = values.astype(F32)
                    squares = squares + wide * wide
                square[...] = squares
                start_tile(1, 0, group)
                return 0

            lax.fori_loop(0, GROUPS, move, 0)
            col = root_scale()
            send_scale(1, col)
            begin_heads(col)

        return 0

    lax.fori_loop(0, STEPS, phase_body, 0)

    col = root_scale()
    last_size = steps_ref[STEPS - 1]

    def put(group, _):
        cols = [head_cols(group * PER + i) for i in range(PER)]
        velocities = [accum[:, c] * col for c in cols]
        moved = [buf[1, pl.ds(0, TOK), c].astype(F32) + last_size * v for c, v in zip(cols, velocities)]
        for c, velocity, denoised in zip(cols, velocities, moved):
            denoised_ref[0, :, c] = denoised.astype(BF16)
            velocity_ref[0, :, c] = velocity.astype(BF16)
        return 0

    lax.fori_loop(0, GROUPS, put, 0)

    def ring_left(number, _):
        for direction in range(2):
            ring_copy(direction, number, False).wait_send()
        return 0

    for number in range(4):
        for direction in range(2):
            ring_copy(direction, number, True).wait_send()
    lax.fori_loop(4, RING, ring_left, 0)
    for which in range(2):
        for half in range(2):
            sib_copy(which, half, 1, True).wait_send()
    each_sibling(3, 7, lambda copy: copy.wait_send())
    for direction in range(2):
        for hop in range(2):
            @pl.when(sends[direction][hop])
            def _():
                for phase in range(STEPS):
                    scale_copy(phase, direction, hop).wait_send()
                    for group in range(GROUPS):
                        tile_copy(phase, direction, hop, group).wait_send()


PIECE = 16
PIECES = TOK // PIECE


def hand_over(denoised_in, velocity_in, denoised_out, velocity_out, sems):
    copies = [
        pltpu.make_async_copy(source.at[0, pl.ds(PIECE * i, PIECE)], target.at[0, pl.ds(PIECE * i, PIECE)], sems.at[which, i])
        for i in range(PIECES)
        for which, (source, target) in enumerate(((denoised_in, denoised_out), (velocity_in, velocity_out)))
    ]
    for copy in copies:
        copy.start()
    for copy in copies:
        copy.wait()


def per_device(latent, past_cache, neighbour_mask, gains, step_sizes):
    dma = pltpu.SemaphoreType.DMA
    hbm = pl.BlockSpec(memory_space=pltpu.HBM)
    vmem = pl.BlockSpec(memory_space=pltpu.VMEM)
    operands = [
        pltpu.with_memory_space_constraint(x, pltpu.HBM)
        for x in (latent, past_cache, neighbour_mask, gains, step_sizes)
    ]
    results = pl.pallas_call(
        kernel,
        out_shape=(pltpu.VMEM((1, TOK, HW), BF16),) * 2,
        in_specs=[hbm] * 5,
        out_specs=(vmem,) * 2,
        scratch_shapes=[
            pltpu.SMEM((1, 1, 4), jnp.int32),
            pltpu.VMEM((2, HW), F32),
            pltpu.SMEM((STEPS,), F32),
            pltpu.VMEM((2, ROWS, HW), BF16),
            pltpu.VMEM((TOK, HW), BF16),
            pltpu.VMEM((TOK, HW), F32),
            pltpu.VMEM((HEADS, TOK, HD), F32),
            pltpu.VMEM((HEADS, TOK, HD), F32),
            pltpu.VMEM((STEPS, 8, HD), F32),
            pltpu.VMEM((STEPS, 4, 8, HD), F32),
            pltpu.VMEM((4 * TOK, HD), F32),
            pltpu.VMEM((5, 8, HD), F32),
            pltpu.VMEM((TOK, HD), F32),
            dma((6,)),
            dma((2, RING)),
            dma((2, 16, 2)),
            dma((2, 16, 2)),
            dma((STEPS, 2, 2, GROUPS)),
            dma((STEPS, 4, GROUPS)),
            dma((STEPS, 2, 2)),
            dma((STEPS, 4)),
        ],
        compiler_params=pltpu.CompilerParams(
            collective_id=0, has_side_effects=True, vmem_limit_bytes=32 * 1024 * 1024
        ),
        cost_estimate=pl.CostEstimate(flops=760_000_000, bytes_accessed=1_200_000, transcendentals=1_600_000),
    )(*operands)
    return pl.pallas_call(
        hand_over,
        out_shape=(jax.ShapeDtypeStruct((1, TOK, HW), BF16),) * 2,
        in_specs=[vmem] * 2,
        out_specs=(hbm,) * 2,
        scratch_shapes=[dma((2, PIECES))],
    )(*(pltpu.with_memory_space_constraint(x, pltpu.VMEM) for x in results))


def solution(mesh):
    in_specs = (P("tm", "space", None), P(None, "tm", "space"), P("tm", "space", None), P(), P())
    out_specs = (P("tm", "space", None), P("tm", "space", None))
    return jax.shard_map(
        per_device, mesh=mesh, in_specs=in_specs, out_specs=out_specs, check_vma=False
    )
```

time: 202 us -> 55.7 us (0.28)
  waiting for transfers between devices: 58.1 us -> 0 us
  local copies, waits for them, and re-layouts: 57.4 us -> 0 us
  Pallas kernels: 0 us -> 55 us
  starting transfers between devices: 34.3 us -> 0 us
  matrix products: 21.5 us -> 0 us
  between operations: 17.3 us -> 0.64 us
  other arithmetic: 12.3 us -> 0 us
    ppermute x8 -> x0, waiting for transfers between devices: 58.1 us -> none  [passed_along(): return lax.ppermute(block, axis, route)]
    pallas_call x0 -> x2, Pallas kernels: none -> 55 us  [the longest x1 54.1 us: per_device(): pl.pallas_call(kernel, out_shape=(pltpu.VMEM((1, TOK, HW), BF16),) * 2, i...]
    ppermute x8 -> x0, starting transfers between devices: 34.2 us -> none  [passed_along(): return lax.ppermute(block, axis, route)]
    dot_general x24 -> x0, matrix products: 21.5 us -> none  [the longest x12 14.7 us: head_scores(): jnp.einsum('thd,nhd->htn', q_heads, k_heads, preferred_element_type=jnp.f...]
    slice x12 -> x0, local copies, waits for them, and re-layouts: 19.7 us -> none  [the longest x8 9.28 us: per_device(): other_values = arrived[1]]
    another operation x16 -> x0, local copies, waits for them, and re-layouts: 18.9 us -> none  [the longest x8 9.94 us: head_scores(): k_heads = keys.reshape(keys.shape[0], HEADS, HD)]
    unnamed x73 -> x0, local copies, waits for them, and re-layouts: 16.6 us -> none
    reduce_sum x12 -> x0, other arithmetic: 5.57 us -> none  [the longest x8 3.22 us: attend(): total = total * factor + jnp.sum(expo, axis=-1)]
  transfers between devices with their start and end apart: 9 -> 0, of which waited for: 5 -> 0; matrix products, arithmetic and copies ran while one was open for 18% -> 0% of each run, Pallas kernels for 0% -> 0%
where the time goes in v1:
time: 55.7 us; the launch traced here: 55.6 us
  Pallas kernels  55 us (99%)
  between operations  0.64 us (1%)
    pallas_call x1, Pallas kernels, per_device(): pl.pallas_call(kernel, out_shape=(pltpu.VMEM((1, TOK, HW), BF16),) * 2, i...  54.1 us

profile of v1, /device:TPU:6, one launch (start us, length us, event | category | flops | bytes accessed | tf_op | source)
XLA Modules:
  0.0 55.6 jit_solution(3779705849874370811)
XLA Ops:
  0.6 54.1 %shard_map.68 = (bf16[1,64,2560]{2,1,0:T(8,128)(2,1)S(1)}, bf16[1,64,2560]{2,1,0:T(8,128)(2,1)S(1)}) custom-call(bf16[1,64,2560]{2,1,0:T(8,128)(2,1)} %latent_hbm.1, bf16[2,16,2560]{2,1,0:T(8,128)(2,1)} %cache_hbm.1, s32[1,1,4]{2,1,0:T(1,128)} %mask_hbm.1, f32[2,2560]{1,0:T(2,128)} %gains_hbm.1, f32[2]{0:T(128)} %steps_hbm.1), custom_call_target="tpu_custom_call" | custom-call | flops 760000000 | bytes 1200000 | tf_op jit(solution)/shard_map/pallas_call | solution.py:479
  54.7 0.9 %shard_map.69 = (bf16[1,64,2560]{2,1,0:T(8,128)(2,1)}, bf16[1,64,2560]{2,1,0:T(8,128)(2,1)}) custom-call(bf16[1,64,2560]{2,1,0:T(8,128)(2,1)S(1)} %get-tuple-element.4.denoised_in, bf16[1,64,2560]{2,1,0:T(8,128)(2,1)S(1)} %get-tuple-element.5.velocity_in), custom_call_target="tpu_custom_call" | custom-call | tf_op jit(solution)/shard_map/pallas_call | solution.py:512

commit v2 on v1

--- a/solution.py
+++ b/solution.py
@@ -72,7 +72,7 @@
         if own:
             src = cache_hbm.at[which, :, half_cols(half)]
         else:
-            src = shard(which, slot(distance - 1, direction), half)
+            src = shard(which, jnp.where(distance == 1, 0, slot(distance - 1, direction)), half)
         return remote(
             src, shard(which, target, half), ysend.at[direction, number], yrecv.at[which, target, half],
             along_y[direction],
@@ -89,9 +89,13 @@
             which, half, distance = ring_place(direction, number)
             ring_copy(direction, number, False).wait_recv()
 
-            @pl.when(number + 4 < RING)
-            def _():
-                ring_copy(direction, number + 4, False).start()
+            @pl.when(number + 1 < RING)
+            def _():
+                ring_copy(direction, number + 1, False).wait_send()
+
+            @pl.when(number + 3 < RING)
+            def _():
+                ring_copy(direction, number + 3, False).start()
 
             sib_copy(which, half, slot(distance, direction) + 1).start()
 
@@ -114,11 +118,11 @@
     def tile_part(phase, number, cols):
         return buf.at[1, tile_rows(phase, number), cols]
 
-    def tile_copy(phase, direction, hop, group):
+    def tile_copy(phase, direction, hop, group, from_hbm=False):
         cols = columns(group)
         if hop == 1:
             src = tile_part(phase, direction, cols)
-        elif isinstance(phase, int) and phase == 0:
+        elif from_hbm:
             src = latent_hbm.at[0, :, cols]
         else:
             src = buf.at[1, pl.ds(0, TOK), cols]
@@ -135,11 +139,17 @@
             src, scale_in.at[phase, target], rsend.at[phase, direction, hop], rrecv.at[phase, target], along_z[direction]
         )
 
-    def start_tile(phase, hop, group):
+    def start_tile(phase, hop, group, from_hbm=False):
         for direction in range(2):
             @pl.when(sends[direction][hop])
             def _():
-                tile_copy(phase, direction, hop, group).start()
+                tile_copy(phase, direction, hop, group, from_hbm).start()
+
+    def tile_left(phase, hop, group):
+        for direction in range(2):
+            @pl.when(sends[direction][hop])
+            def _():
+                tile_copy(phase, direction, hop, group).wait_send()
 
     def wait_tile(phase, hop, group):
         for direction in range(2):
@@ -148,7 +158,24 @@
                 tile_copy(phase, direction, hop, group).wait_recv()
 
         if hop == 0:
-            start_tile(phase, 1, group)
+            @pl.when(group < GROUPS - 1)
+            def _():
+                tile_left(phase, 0, group + 1)
+
+            @pl.when(group == GROUPS - 1)
+            def _():
+                tile_left(phase, 1, 0)
+
+            @pl.when(group == 0)
+            def _():
+                start_tile(phase, 0, GROUPS - 1)
+
+            @pl.when(group > 0)
+            def _():
+                start_tile(phase, 1, group - 1)
+        elif group == 0:
+            tile_left(phase, 1, 1)
+            start_tile(phase, 1, GROUPS - 1)
 
     diagonal = lax.broadcasted_iota(jnp.int32, (TOK, HD), 0) == lax.broadcasted_iota(jnp.int32, (TOK, HD), 1)
 
@@ -267,10 +294,8 @@
     for number in range(2):
         for direction in range(2):
             ring_copy(direction, number, True).start()
-    start_tile(0, 0, 0)
-    for number in range(2, 4):
-        for direction in range(2):
-            ring_copy(direction, number, True).start()
+    for group in range(2):
+        start_tile(0, 0, group, True)
     for which in range(2):
         for half in range(2):
             sib_copy(which, half, 1, True).start()
@@ -315,11 +340,12 @@
     lax.fori_loop(0, GROUPS, add_squares, 0)
     col = root_scale()
     send_scale(0, col)
-    for group in range(1, GROUPS):
-        start_tile(0, 0, group)
-    begin_heads(col)
     for load in loads[1:3]:
         load.wait()
+    for direction in range(2):
+        ring_copy(direction, 0, True).wait_send()
+        ring_copy(direction, 2, False).start()
+    begin_heads(col)
 
     def phase_body(phase, _):
         first = phase == 0
@@ -349,6 +375,13 @@
             lax.fori_loop(0, HEADS // BATCH, body, 0)
 
         stored(0)
+        tile_left(phase, 0, 0)
+        start_tile(phase, 0, 2)
+
+        @pl.when(jnp.logical_not(first))
+        def _():
+            stored(1)
+            stored(2)
 
         def near(part, _):
             arrive(0, 2 * part)
@@ -366,8 +399,8 @@
         @pl.when(first)
         def _():
             each_sibling(3, 4, lambda copy: copy.wait_recv())
-
-        stored(1)
+            stored(1)
+
         arrive(1, 0)
         take_scales(phase, 1)
         arrive(1, 1)
@@ -378,8 +411,8 @@
         @pl.when(first)
         def _():
             each_sibling(11, 3, lambda copy: copy.wait_recv())
-
-        stored(2)
+            stored(2)
+
         lax.fori_loop(0, 3, finish, 0)
         arrive(1, 3, rounds=False)
         update(FAR, phase, heads_of(3, PER))
@@ -403,7 +436,11 @@
                     wide = values.astype(F32)
                     squares = squares + wide * wide
                 square[...] = squares
-                start_tile(1, 0, group)
+
+                @pl.when(group < 2)
+                def _():
+                    start_tile(1, 0, group)
+
                 return 0
 
             lax.fori_loop(0, GROUPS, move, 0)
@@ -429,27 +466,19 @@
 
     lax.fori_loop(0, GROUPS, put, 0)
 
-    def ring_left(number, _):
-        for direction in range(2):
-            ring_copy(direction, number, False).wait_send()
-        return 0
-
-    for number in range(4):
-        for direction in range(2):
-            ring_copy(direction, number, True).wait_send()
-    lax.fori_loop(4, RING, ring_left, 0)
     for which in range(2):
         for half in range(2):
             sib_copy(which, half, 1, True).wait_send()
     each_sibling(3, 7, lambda copy: copy.wait_send())
-    for direction in range(2):
-        for hop in range(2):
-            @pl.when(sends[direction][hop])
-            def _():
-                for phase in range(STEPS):
+    for phase in range(STEPS):
+        for direction in range(2):
+            for hop in range(2):
+                @pl.when(sends[direction][hop])
+                def _():
                     scale_copy(phase, direction, hop).wait_send()
-                    for group in range(GROUPS):
-                        tile_copy(phase, direction, hop, group).wait_send()
+
+        for group in range(2, GROUPS):
+            tile_left(phase, 1, group)
 
 
 PIECE = 16

time: 55.7 us -> 57.3 us (1.029)
  Pallas kernels: 55 us -> 56.5 us
    pallas_call x1, Pallas kernels: 54.1 us -> 55.6 us  [per_device(): pl.pallas_call(kernel, out_shape=(pltpu.VMEM((1, TOK, HW), BF16),) * 2, i...]
where the time goes in v2:
time: 57.3 us; the launch traced here: 57.1 us
  Pallas kernels  56.5 us (99%)
  between operations  0.64 us (1%)
    pallas_call x1, Pallas kernels, per_device(): pl.pallas_call(kernel, out_shape=(pltpu.VMEM((1, TOK, HW), BF16),) * 2, i...  55.6 us

profile of v2, /device:TPU:6, one launch (start us, length us, event | category | flops | bytes accessed | tf_op | source)
XLA Modules:
  0.0 57.1 jit_solution(11816133744568168191)
XLA Ops:
  0.6 55.6 %shard_map.68 = (bf16[1,64,2560]{2,1,0:T(8,128)(2,1)S(1)}, bf16[1,64,2560]{2,1,0:T(8,128)(2,1)S(1)}) custom-call(bf16[1,64,2560]{2,1,0:T(8,128)(2,1)} %latent_hbm.1, bf16[2,16,2560]{2,1,0:T(8,128)(2,1)} %cache_hbm.1, s32[1,1,4]{2,1,0:T(1,128)} %mask_hbm.1, f32[2,2560]{1,0:T(2,128)} %gains_hbm.1, f32[2]{0:T(128)} %steps_hbm.1), custom_call_target="tpu_custom_call" | custom-call | flops 760000000 | bytes 1200000 | tf_op jit(solution)/shard_map/pallas_call | solution.py:508
  56.3 0.9 %shard_map.69 = (bf16[1,64,2560]{2,1,0:T(8,128)(2,1)}, bf16[1,64,2560]{2,1,0:T(8,128)(2,1)}) custom-call(bf16[1,64,2560]{2,1,0:T(8,128)(2,1)S(1)} %get-tuple-element.4.denoised_in, bf16[1,64,2560]{2,1,0:T(8,128)(2,1)S(1)} %get-tuple-element.5.velocity_in), custom_call_target="tpu_custom_call" | custom-call | tf_op jit(solution)/shard_map/pallas_call | solution.py:541

commit v3 on v1

--- a/solution.py
+++ b/solution.py
@@ -328,14 +328,11 @@
         def heads_of(part, count):
             return [part * count + i for i in range(count)]
 
-        def arrive(hop, group, rounds=True):
-            if rounds:
-                @pl.when(first)
-                def _():
-                    ring_round(8 * hop + 2 * group)
-                    ring_round(8 * hop + 2 * group + 1)
-
-            wait_tile(phase, hop, group)
+        def rounds(start, count):
+            @pl.when(first)
+            def _():
+                for number in range(count):
+                    ring_round(start + number)
 
         @pl.when(first)
         def _():
@@ -350,14 +347,25 @@
 
         stored(0)
 
+        @pl.when(jnp.logical_not(first))
+        def _():
+            stored(1)
+            stored(2)
+
         def near(part, _):
-            arrive(0, 2 * part)
+            for i in range(2):
+                group = 2 * part + i
+                rounds(2 * group, 2)
+                wait_tile(phase, 0, group)
 
             @pl.when(part == 0)
             def _():
                 take_scales(phase, 0)
 
-            arrive(0, 2 * part + 1)
+            @pl.when(part == 1)
+            def _():
+                rounds(8, 2)
+
             update(NEAR, phase, heads_of(part, 2 * PER))
             return 0
 
@@ -366,22 +374,24 @@
         @pl.when(first)
         def _():
             each_sibling(3, 4, lambda copy: copy.wait_recv())
-
-        stored(1)
-        arrive(1, 0)
+            stored(1)
+
+        rounds(10, 2)
+        wait_tile(phase, 1, 0)
+        wait_tile(phase, 1, 1)
         take_scales(phase, 1)
-        arrive(1, 1)
         update(FAR, phase, heads_of(0, 2 * PER))
-        arrive(1, 2)
+        rounds(12, 2)
+        wait_tile(phase, 1, 2)
         update(FAR, phase, heads_of(2, PER))
 
         @pl.when(first)
         def _():
             each_sibling(11, 3, lambda copy: copy.wait_recv())
-
-        stored(2)
+            stored(2)
+
         lax.fori_loop(0, 3, finish, 0)
-        arrive(1, 3, rounds=False)
+        wait_tile(phase, 1, 3)
         update(FAR, phase, heads_of(3, PER))
         finish(3, 0)
 
@@ -403,12 +413,18 @@
                     wide = values.astype(F32)
                     squares = squares + wide * wide
                 square[...] = squares
-                start_tile(1, 0, group)
+
+                @pl.when(group == 0)
+                def _():
+                    start_tile(1, 0, 0)
+
                 return 0
 
             lax.fori_loop(0, GROUPS, move, 0)
             col = root_scale()
             send_scale(1, col)
+            for group in range(1, GROUPS):
+                start_tile(1, 0, group)
             begin_heads(col)
 
         return 0

time: 55.7 us -> 54 us (0.969)
  Pallas kernels: 55 us -> 53 us
    pallas_call x1, Pallas kernels: 54.1 us -> 52.1 us  [per_device(): pl.pallas_call(kernel, out_shape=(pltpu.VMEM((1, TOK, HW), BF16),) * 2, i...]
where the time goes in v3:
time: 54 us; the launch traced here: 53.6 us
  Pallas kernels  53 us (98%)
  between operations  0.64 us (1%)
    pallas_call x1, Pallas kernels, per_device(): pl.pallas_call(kernel, out_shape=(pltpu.VMEM((1, TOK, HW), BF16),) * 2, i...  52.1 us

profile of v3, /device:TPU:6, one launch (start us, length us, event | category | flops | bytes accessed | tf_op | source)
XLA Modules:
  0.0 53.6 jit_solution(2888317046971443166)
XLA Ops:
  0.6 52.1 %shard_map.68 = (bf16[1,64,2560]{2,1,0:T(8,128)(2,1)S(1)}, bf16[1,64,2560]{2,1,0:T(8,128)(2,1)S(1)}) custom-call(bf16[1,64,2560]{2,1,0:T(8,128)(2,1)} %latent_hbm.1, bf16[2,16,2560]{2,1,0:T(8,128)(2,1)} %cache_hbm.1, s32[1,1,4]{2,1,0:T(1,128)} %mask_hbm.1, f32[2,2560]{1,0:T(2,128)} %gains_hbm.1, f32[2]{0:T(128)} %steps_hbm.1), custom_call_target="tpu_custom_call" | custom-call | flops 760000000 | bytes 1200000 | tf_op jit(solution)/shard_map/pallas_call | solution.py:495
  52.7 0.9 %shard_map.69 = (bf16[1,64,2560]{2,1,0:T(8,128)(2,1)}, bf16[1,64,2560]{2,1,0:T(8,128)(2,1)}) custom-call(bf16[1,64,2560]{2,1,0:T(8,128)(2,1)S(1)} %get-tuple-element.4.denoised_in, bf16[1,64,2560]{2,1,0:T(8,128)(2,1)S(1)} %get-tuple-element.5.velocity_in), custom_call_target="tpu_custom_call" | custom-call | tf_op jit(solution)/shard_map/pallas_call | solution.py:528

commit v4 on v3

--- a/solution.py
+++ b/solution.py
@@ -16,7 +16,6 @@
 GROUPS = 4
 PER = HEADS // GROUPS
 GW = PER * HD
-BATCH = 20
 EPS = 1e-6
 SCORE_SCALE = math.log2(math.e) / math.sqrt(HD)
 MASKED = -1e30
@@ -106,6 +105,8 @@
         return pl.ds(pl.multiple_of(group * GW, GW), GW)
 
     def head_cols(head):
+        if isinstance(head, int):
+            return pl.ds(head * HD, HD)
         return pl.ds(pl.multiple_of(head * HD, HD), HD)
 
     def tile_rows(phase, number):
@@ -234,15 +235,42 @@
             total[head] = totals[i]
             accum[:, cols[i]] = sums[i]
 
-    def finish(group, _):
-        heads = [group * PER + i for i in range(PER)]
+    def finish(heads):
+        attended = [accum[:, head_cols(head)] / jnp.sum(total[head], axis=1, keepdims=True) for head in heads]
         squares = square[...]
-        attended = [accum[:, head_cols(head)] / jnp.sum(total[head], axis=1, keepdims=True) for head in heads]
         for head, values in zip(heads, attended):
             accum[:, head_cols(head)] = values
             squares = squares + values * values
         square[...] = squares
-        return 0
+
+    def tiles_left(phase, hop):
+        for direction in range(2):
+            @pl.when(sends[direction][hop])
+            def _():
+                scale_copy(phase, direction, hop).wait_send()
+
+                def body(group, _):
+                    tile_copy(phase, direction, hop, group).wait_send()
+                    return 0
+
+                lax.fori_loop(0, GROUPS, body, 0)
+
+    def earlier_sends_left():
+        def ring_left(number, _):
+            for direction in range(2):
+                ring_copy(direction, number, False).wait_send()
+            return 0
+
+        for number in range(4):
+            for direction in range(2):
+                ring_copy(direction, number, True).wait_send()
+        lax.fori_loop(4, RING, ring_left, 0)
+        for which in range(2):
+            for half in range(2):
+                sib_copy(which, half, 1, True).wait_send()
+        each_sibling(3, 7, lambda copy: copy.wait_send())
+        for hop in range(2):
+            tiles_left(0, hop)
 
     loads = [
         pltpu.make_async_copy(latent_hbm.at[0], buf.at[1, pl.ds(0, TOK)], local_sem.at[0]),
@@ -339,11 +367,7 @@
             each_sibling(1, 1, lambda copy: copy.wait_recv())
 
         def stored(stage):
-            def body(part, _):
-                update(stage, phase, heads_of(part, BATCH))
-                return 0
-
-            lax.fori_loop(0, HEADS // BATCH, body, 0)
+            update(stage, phase, heads_of(0, HEADS))
 
         stored(0)
 
@@ -375,6 +399,10 @@
         def _():
             each_sibling(3, 4, lambda copy: copy.wait_recv())
             stored(1)
+
+        @pl.when(jnp.logical_not(first))
+        def _():
+            earlier_sends_left()
 
         rounds(10, 2)
         wait_tile(phase, 1, 0)
@@ -387,13 +415,16 @@
 
         @pl.when(first)
         def _():
-            each_sibling(11, 3, lambda copy: copy.wait_recv())
-            stored(2)
-
-        lax.fori_loop(0, 3, finish, 0)
+            for half in range(2):
+                for target in (11, 13, 15):
+                    for which in range(2):
+                        sib_copy(which, half, target).wait_recv()
+                update(2, phase, heads_of(half, HEADS // 2))
+
+        finish(heads_of(0, 3 * PER))
         wait_tile(phase, 1, 3)
         update(FAR, phase, heads_of(3, PER))
-        finish(3, 0)
+        finish(heads_of(3, PER))
 
         @pl.when(first)
         def _():
@@ -434,38 +465,15 @@
     col = root_scale()
     last_size = steps_ref[STEPS - 1]
 
-    def put(group, _):
-        cols = [head_cols(group * PER + i) for i in range(PER)]
-        velocities = [accum[:, c] * col for c in cols]
-        moved = [buf[1, pl.ds(0, TOK), c].astype(F32) + last_size * v for c, v in zip(cols, velocities)]
-        for c, velocity, denoised in zip(cols, velocities, moved):
-            denoised_ref[0, :, c] = denoised.astype(BF16)
-            velocity_ref[0, :, c] = velocity.astype(BF16)
-        return 0
-
-    lax.fori_loop(0, GROUPS, put, 0)
-
-    def ring_left(number, _):
-        for direction in range(2):
-            ring_copy(direction, number, False).wait_send()
-        return 0
-
-    for number in range(4):
-        for direction in range(2):
-            ring_copy(direction, number, True).wait_send()
-    lax.fori_loop(4, RING, ring_left, 0)
-    for which in range(2):
-        for half in range(2):
-            sib_copy(which, half, 1, True).wait_send()
-    each_sibling(3, 7, lambda copy: copy.wait_send())
-    for direction in range(2):
-        for hop in range(2):
-            @pl.when(sends[direction][hop])
-            def _():
-                for phase in range(STEPS):
-                    scale_copy(phase, direction, hop).wait_send()
-                    for group in range(GROUPS):
-                        tile_copy(phase, direction, hop, group).wait_send()
+    cols = [head_cols(head) for head in range(HEADS)]
+    velocities = [accum[:, c] * col for c in cols]
+    moved = [buf[1, pl.ds(0, TOK), c].astype(F32) + last_size * v for c, v in zip(cols, velocities)]
+    for c, velocity, denoised in zip(cols, velocities, moved):
+        denoised_ref[0, :, c] = denoised.astype(BF16)
+        velocity_ref[0, :, c] = velocity.astype(BF16)
+
+    for hop in range(2):
+        tiles_left(1, hop)
 
 
 PIECE = 16

time: 54 us -> 52.8 us (0.978)
  Pallas kernels: 53 us -> 52 us
    pallas_call x1, Pallas kernels: 52.1 us -> 51.1 us  [per_device(): pl.pallas_call(kernel, out_shape=(pltpu.VMEM((1, TOK, HW), BF16),) * 2, i...]
where the time goes in v4:
time: 52.8 us; the launch traced here: 52.7 us
  Pallas kernels  52 us (98%)
  between operations  0.64 us (1%)
    pallas_call x1, Pallas kernels, per_device(): pl.pallas_call(kernel, out_shape=(pltpu.VMEM((1, TOK, HW), BF16),) * 2, i...  51.1 us

profile of v4, /device:TPU:6, one launch (start us, length us, event | category | flops | bytes accessed | tf_op | source)
XLA Modules:
  0.0 52.7 jit_solution(1320437225802842141)
XLA Ops:
  0.6 51.1 %shard_map.68 = (bf16[1,64,2560]{2,1,0:T(8,128)(2,1)S(1)}, bf16[1,64,2560]{2,1,0:T(8,128)(2,1)S(1)}) custom-call(bf16[1,64,2560]{2,1,0:T(8,128)(2,1)} %latent_hbm.1, bf16[2,16,2560]{2,1,0:T(8,128)(2,1)} %cache_hbm.1, s32[1,1,4]{2,1,0:T(1,128)} %mask_hbm.1, f32[2,2560]{1,0:T(2,128)} %gains_hbm.1, f32[2]{0:T(128)} %steps_hbm.1), custom_call_target="tpu_custom_call" | custom-call | flops 760000000 | bytes 1200000 | tf_op jit(solution)/shard_map/pallas_call | solution.py:503
  51.8 0.9 %shard_map.69 = (bf16[1,64,2560]{2,1,0:T(8,128)(2,1)}, bf16[1,64,2560]{2,1,0:T(8,128)(2,1)}) custom-call(bf16[1,64,2560]{2,1,0:T(8,128)(2,1)S(1)} %get-tuple-element.4.denoised_in, bf16[1,64,2560]{2,1,0:T(8,128)(2,1)S(1)} %get-tuple-element.5.velocity_in), custom_call_target="tpu_custom_call" | custom-call | tf_op jit(solution)/shard_map/pallas_call | solution.py:536

commit v5 on v4

--- a/solution.py
+++ b/solution.py
@@ -1,3 +1,4 @@
+import functools
 import math
 
 import jax
@@ -197,40 +198,43 @@
 
         lax.fori_loop(0, GROUPS, body, 0)
 
-    def tile_keys(stage, phase, heads):
-        scales = scale_col[pl.ds(pl.multiple_of((stage - NEAR) * STAGE, STAGE), STAGE), :]
-        source = pl.ds(pl.multiple_of((stage + phase * 2) * STAGE, STAGE), STAGE)
-        return [
-            (buf[1, source, head_cols(head)].astype(F32) * scales * gains_ref[1:2, head_cols(head)]).astype(BF16)
-            for head in heads
+    def keys_values(head, stage, phase):
+        cols = head_cols(head)
+        if stage < NEAR:
+            rows = pl.ds(stage * STAGE, STAGE)
+            return buf[0, rows, cols], buf[1, rows, cols]
+        values = buf[1, pl.ds(pl.multiple_of((stage + phase * 2) * STAGE, STAGE), STAGE), cols]
+        scales = scale_col[pl.ds((stage - NEAR) * STAGE, STAGE), :]
+        return (values.astype(F32) * scales * gains_ref[1:2, cols]).astype(BF16), values
+
+    def update(phase, *parts):
+        plan = [(head, stages) for heads, stages in parts for head in heads]
+        cols = [head_cols(head) for head, _ in plan]
+        tiles = [[keys_values(head, stage, phase) for stage in stages] for head, stages in plan]
+        queries = [query[:, c] for c in cols]
+        old_peaks = [peak[head] for head, _ in plan]
+        scores = [
+            [
+                lax.dot_general(q, k, (((1,), (1,)), ((), ())), preferred_element_type=F32) * SCORE_SCALE
+                + bias[stage, 0:1, :]
+                for stage, (k, _) in zip(stages, pairs)
+            ]
+            for q, pairs, (_, stages) in zip(queries, tiles, plan)
         ]
-
-    def update(stage, phase, heads):
-        cols = [head_cols(head) for head in heads]
-        value_stage = stage + phase * 2 if stage >= NEAR else stage
-        value_rows = pl.ds(pl.multiple_of(value_stage * STAGE, STAGE), STAGE)
-        allowed = bias[stage, 0:1, :]
-        if stage >= NEAR:
-            keys = tile_keys(stage, phase, heads)
-        else:
-            keys = [buf[0, value_rows, c] for c in cols]
-        queries = [query[:, c] for c in cols]
-        old_peaks = [peak[head] for head in heads]
-        scores = [
-            lax.dot_general(q, k, (((1,), (1,)), ((), ())), preferred_element_type=F32) * SCORE_SCALE + allowed
-            for q, k in zip(queries, keys)
+        tops = [functools.reduce(jnp.maximum, each) for each in scores]
+        peaks = [
+            jnp.maximum(old, jnp.broadcast_to(jnp.max(top, axis=1, keepdims=True), (TOK, HD)))
+            for old, top in zip(old_peaks, tops)
         ]
-        peaks = [
-            jnp.maximum(old, jnp.broadcast_to(jnp.max(s, axis=1, keepdims=True), (TOK, HD)))
-            for old, s in zip(old_peaks, scores)
+        expos = [[jnp.exp2(s - p) for s in each] for each, p in zip(scores, peaks)]
+        mixed = [
+            sum(jnp.dot(e.astype(BF16), v, preferred_element_type=F32) for e, (_, v) in zip(each, pairs))
+            for each, pairs in zip(expos, tiles)
         ]
-        expos = [jnp.exp2(s - p) for s, p in zip(scores, peaks)]
-        values = [buf[1, value_rows, c] for c in cols]
-        mixed = [jnp.dot(e.astype(BF16), v, preferred_element_type=F32) for e, v in zip(expos, values)]
         factors = [jnp.exp2(old - new) for old, new in zip(old_peaks, peaks)]
-        totals = [total[head] * f + e for head, f, e in zip(heads, factors, expos)]
+        totals = [total[head] * f + sum(each) for (head, _), f, each in zip(plan, factors, expos)]
         sums = [accum[:, c] * f + m for c, f, m in zip(cols, factors, mixed)]
-        for i, head in enumerate(heads):
+        for i, (head, _) in enumerate(plan):
             peak[head] = peaks[i]
             total[head] = totals[i]
             accum[:, cols[i]] = sums[i]
@@ -353,52 +357,41 @@
         first = phase == 0
         square[...] = jnp.zeros((TOK, HD), F32)
 
-        def heads_of(part, count):
-            return [part * count + i for i in range(count)]
-
         def rounds(start, count):
             @pl.when(first)
             def _():
-                for number in range(count):
-                    ring_round(start + number)
+                for number in range(start, start + count):
+                    ring_round(number)
+
+        def last_shards(half):
+            for target in (11, 13, 15):
+                for which in range(2):
+                    sib_copy(which, half, target).wait_recv()
+
+        every = range(HEADS)
 
         @pl.when(first)
         def _():
             each_sibling(1, 1, lambda copy: copy.wait_recv())
 
-        def stored(stage):
-            update(stage, phase, heads_of(0, HEADS))
-
-        stored(0)
+        update(phase, (every, (0,)))
 
         @pl.when(jnp.logical_not(first))
         def _():
-            stored(1)
-            stored(2)
-
-        def near(part, _):
-            for i in range(2):
-                group = 2 * part + i
-                rounds(2 * group, 2)
-                wait_tile(phase, 0, group)
-
-            @pl.when(part == 0)
-            def _():
-                take_scales(phase, 0)
-
-            @pl.when(part == 1)
-            def _():
-                rounds(8, 2)
-
-            update(NEAR, phase, heads_of(part, 2 * PER))
-            return 0
-
-        lax.fori_loop(0, GROUPS // 2, near, 0)
+            update(phase, (every, (1,)))
+            update(phase, (every, (2,)))
+
+        for group in range(GROUPS):
+            rounds(2 * group, 2)
+            wait_tile(phase, 0, group)
+        rounds(8, 2)
+        take_scales(phase, 0)
+        update(phase, (every, (NEAR,)))
 
         @pl.when(first)
         def _():
             each_sibling(3, 4, lambda copy: copy.wait_recv())
-            stored(1)
+            update(phase, (every, (1,)))
 
         @pl.when(jnp.logical_not(first))
         def _():
@@ -408,23 +401,27 @@
         wait_tile(phase, 1, 0)
         wait_tile(phase, 1, 1)
         take_scales(phase, 1)
-        update(FAR, phase, heads_of(0, 2 * PER))
+        update(phase, (every[:2 * PER], (FAR,)))
         rounds(12, 2)
         wait_tile(phase, 1, 2)
-        update(FAR, phase, heads_of(2, PER))
+        update(phase, (every[2 * PER : 3 * PER], (FAR,)))
 
         @pl.when(first)
         def _():
-            for half in range(2):
-                for target in (11, 13, 15):
-                    for which in range(2):
-                        sib_copy(which, half, target).wait_recv()
-                update(2, phase, heads_of(half, HEADS // 2))
-
-        finish(heads_of(0, 3 * PER))
-        wait_tile(phase, 1, 3)
-        update(FAR, phase, heads_of(3, PER))
-        finish(heads_of(3, PER))
+            last_shards(0)
+            update(phase, (every[: 2 * PER], (2,)))
+            finish(every[: 2 * PER])
+            last_shards(1)
+            wait_tile(phase, 1, 3)
+            update(phase, (every[2 * PER : 3 * PER], (2,)), (every[3 * PER :], (2, FAR)))
+            finish(every[2 * PER :])
+
+        @pl.when(jnp.logical_not(first))
+        def _():
+            finish(every[: 3 * PER])
+            wait_tile(phase, 1, 3)
+            update(phase, (every[3 * PER :], (FAR,)))
+            finish(every[3 * PER :])
 
         @pl.when(first)
         def _():

time: 52.8 us -> 54.6 us (1.034)
  Pallas kernels: 52 us -> 53.6 us
    pallas_call x1, Pallas kernels: 51.1 us -> 52.7 us  [per_device(): pl.pallas_call(kernel, out_shape=(pltpu.VMEM((1, TOK, HW), BF16),) * 2, i...]
where the time goes in v5:
time: 54.6 us; the launch traced here: 54.2 us
  Pallas kernels  53.6 us (98%)
  between operations  0.64 us (1%)
    pallas_call x1, Pallas kernels, per_device(): pl.pallas_call(kernel, out_shape=(pltpu.VMEM((1, TOK, HW), BF16),) * 2, i...  52.7 us

profile of v5, /device:TPU:6, one launch (start us, length us, event | category | flops | bytes accessed | tf_op | source)
XLA Modules:
  0.0 54.2 jit_solution(16918912133362382125)
XLA Ops:
  0.6 52.7 %shard_map.68 = (bf16[1,64,2560]{2,1,0:T(8,128)(2,1)S(1)}, bf16[1,64,2560]{2,1,0:T(8,128)(2,1)S(1)}) custom-call(bf16[1,64,2560]{2,1,0:T(8,128)(2,1)} %latent_hbm.1, bf16[2,16,2560]{2,1,0:T(8,128)(2,1)} %cache_hbm.1, s32[1,1,4]{2,1,0:T(1,128)} %mask_hbm.1, f32[2,2560]{1,0:T(2,128)} %gains_hbm.1, f32[2]{0:T(128)} %steps_hbm.1), custom_call_target="tpu_custom_call" | custom-call | flops 760000000 | bytes 1200000 | tf_op jit(solution)/shard_map/pallas_call | solution.py:500
  53.3 0.9 %shard_map.69 = (bf16[1,64,2560]{2,1,0:T(8,128)(2,1)}, bf16[1,64,2560]{2,1,0:T(8,128)(2,1)}) custom-call(bf16[1,64,2560]{2,1,0:T(8,128)(2,1)S(1)} %get-tuple-element.4.denoised_in, bf16[1,64,2560]{2,1,0:T(8,128)(2,1)S(1)} %get-tuple-element.5.velocity_in), custom_call_target="tpu_custom_call" | custom-call | tf_op jit(solution)/shard_map/pallas_call | solution.py:533

commit v6 on v5

--- a/solution.py
+++ b/solution.py
@@ -198,41 +198,62 @@
 
         lax.fori_loop(0, GROUPS, body, 0)
 
-    def keys_values(head, stage, phase):
+    def value_rows(stage, count, phase):
+        start = (stage + phase * 2) * STAGE if stage >= NEAR else stage * STAGE
+        return pl.ds(pl.multiple_of(start, STAGE), count * STAGE)
+
+    def keys_of(head, stage, count, phase):
         cols = head_cols(head)
+        rows = value_rows(stage, count, phase)
         if stage < NEAR:
-            rows = pl.ds(stage * STAGE, STAGE)
-            return buf[0, rows, cols], buf[1, rows, cols]
-        values = buf[1, pl.ds(pl.multiple_of((stage + phase * 2) * STAGE, STAGE), STAGE), cols]
+            return buf[0, rows, cols]
         scales = scale_col[pl.ds((stage - NEAR) * STAGE, STAGE), :]
-        return (values.astype(F32) * scales * gains_ref[1:2, cols]).astype(BF16), values
+        return (buf[1, rows, cols].astype(F32) * scales * gains_ref[1:2, cols]).astype(BF16)
+
+    def mix(plan, weights, phase):
+        mixed = []
+        at = 0
+        while at < len(plan):
+            head, spans = plan[at]
+            pair = 2 if at + 1 < len(plan) and plan[at + 1] == (head + 1, spans) else 1
+            cols = pl.ds(head * HD, pair * HD)
+            sums = None
+            for i, (stage, count) in enumerate(spans):
+                stacked = jnp.concatenate([weights[at + j][i] for j in range(pair)], axis=0)
+                product = jnp.dot(stacked, buf[1, value_rows(stage, count, phase), cols], preferred_element_type=F32)
+                sums = product if sums is None else sums + product
+            mixed += [sums[j * TOK : (j + 1) * TOK, j * HD : (j + 1) * HD] for j in range(pair)]
+            at += pair
+        return mixed
 
     def update(phase, *parts):
-        plan = [(head, stages) for heads, stages in parts for head in heads]
+        plan = [(head, spans) for heads, spans in parts for head in heads]
         cols = [head_cols(head) for head, _ in plan]
-        tiles = [[keys_values(head, stage, phase) for stage in stages] for head, stages in plan]
+        keys = [[keys_of(head, stage, count, phase) for stage, count in spans] for head, spans in plan]
         queries = [query[:, c] for c in cols]
         old_peaks = [peak[head] for head, _ in plan]
-        scores = [
-            [
-                lax.dot_general(q, k, (((1,), (1,)), ((), ())), preferred_element_type=F32) * SCORE_SCALE
-                + bias[stage, 0:1, :]
-                for stage, (k, _) in zip(stages, pairs)
-            ]
-            for q, pairs, (_, stages) in zip(queries, tiles, plan)
-        ]
-        tops = [functools.reduce(jnp.maximum, each) for each in scores]
+        scores = []
+        for q, each, (_, spans) in zip(queries, keys, plan):
+            pieces = []
+            for k, (stage, count) in zip(each, spans):
+                raw = lax.dot_general(q, k, (((1,), (1,)), ((), ())), preferred_element_type=F32)
+                pieces.append([
+                    raw[:, i * STAGE : (i + 1) * STAGE] * SCORE_SCALE + bias[stage + i, 0:1, :] for i in range(count)
+                ])
+            scores.append(pieces)
+        tops = [functools.reduce(jnp.maximum, sum(pieces, [])) for pieces in scores]
         peaks = [
             jnp.maximum(old, jnp.broadcast_to(jnp.max(top, axis=1, keepdims=True), (TOK, HD)))
             for old, top in zip(old_peaks, tops)
         ]
-        expos = [[jnp.exp2(s - p) for s in each] for each, p in zip(scores, peaks)]
-        mixed = [
-            sum(jnp.dot(e.astype(BF16), v, preferred_element_type=F32) for e, (_, v) in zip(each, pairs))
-            for each, pairs in zip(expos, tiles)
+        expos = [[[jnp.exp2(s - p) for s in span] for span in pieces] for pieces, p in zip(scores, peaks)]
+        weights = [[jnp.concatenate([e.astype(BF16) for e in span], axis=1) for span in each] for each in expos]
+        mixed = mix(plan, weights, phase)
+        factors = [jnp.exp2(old - new) for old, new in zip(old_peaks, peaks)]
+        totals = [
+            total[head] * f + functools.reduce(jnp.add, sum(each, []))
+            for (head, _), f, each in zip(plan, factors, expos)
         ]
-        factors = [jnp.exp2(old - new) for old, new in zip(old_peaks, peaks)]
-        totals = [total[head] * f + sum(each) for (head, _), f, each in zip(plan, factors, expos)]
         sums = [accum[:, c] * f + m for c, f, m in zip(cols, factors, mixed)]
         for i, (head, _) in enumerate(plan):
             peak[head] = peaks[i]
@@ -374,24 +395,33 @@
         def _():
             each_sibling(1, 1, lambda copy: copy.wait_recv())
 
-        update(phase, (every, (0,)))
+        @pl.when(first)
+        def _():
+            update(phase, (every, ((0, 1),)))
 
         @pl.when(jnp.logical_not(first))
         def _():
-            update(phase, (every, (1,)))
-            update(phase, (every, (2,)))
-
-        for group in range(GROUPS):
+            update(phase, (every[: 2 * PER], ((0, 3),)))
+            update(phase, (every[2 * PER :], ((0, 3),)))
+
+        near, far = ((NEAR, 1),), ((FAR, 1),)
+        for group in range(2):
             rounds(2 * group, 2)
             wait_tile(phase, 0, group)
+        take_scales(phase, 0)
+        update(phase, (every[: 2 * PER], near))
+        rounds(4, 2)
+        wait_tile(phase, 0, 2)
+        update(phase, (every[2 * PER : 3 * PER], near))
+        rounds(6, 2)
+        wait_tile(phase, 0, 3)
         rounds(8, 2)
-        take_scales(phase, 0)
-        update(phase, (every, (NEAR,)))
+        update(phase, (every[3 * PER :], near))
 
         @pl.when(first)
         def _():
             each_sibling(3, 4, lambda copy: copy.wait_recv())
-            update(phase, (every, (1,)))
+            update(phase, (every, ((1, 1),)))
 
         @pl.when(jnp.logical_not(first))
         def _():
@@ -401,26 +431,26 @@
         wait_tile(phase, 1, 0)
         wait_tile(phase, 1, 1)
         take_scales(phase, 1)
-        update(phase, (every[:2 * PER], (FAR,)))
+        update(phase, (every[: 2 * PER], far))
         rounds(12, 2)
         wait_tile(phase, 1, 2)
-        update(phase, (every[2 * PER : 3 * PER], (FAR,)))
+        update(phase, (every[2 * PER : 3 * PER], far))
 
         @pl.when(first)
         def _():
             last_shards(0)
-            update(phase, (every[: 2 * PER], (2,)))
+            update(phase, (every[: 2 * PER], ((2, 1),)))
             finish(every[: 2 * PER])
             last_shards(1)
             wait_tile(phase, 1, 3)
-            update(phase, (every[2 * PER : 3 * PER], (2,)), (every[3 * PER :], (2, FAR)))
+            update(phase, (every[2 * PER : 3 * PER], ((2, 1),)), (every[3 * PER :], ((2, 1), (FAR, 1))))
             finish(every[2 * PER :])
 
         @pl.when(jnp.logical_not(first))
         def _():
             finish(every[: 3 * PER])
             wait_tile(phase, 1, 3)
-            update(phase, (every[3 * PER :], (FAR,)))
+            update(phase, (every[3 * PER :], far))
             finish(every[3 * PER :])
 
         @pl.when(first)

time: 54.6 us -> 52.3 us (0.958)
  Pallas kernels: 53.6 us -> 51.5 us
    pallas_call x1, Pallas kernels: 52.7 us -> 50.6 us  [per_device(): pl.pallas_call(kernel, out_shape=(pltpu.VMEM((1, TOK, HW), BF16),) * 2, i...]
where the time goes in v6:
time: 52.3 us; the launch traced here: 52.2 us
  Pallas kernels  51.5 us (98%)
  between operations  0.64 us (1%)
    pallas_call x1, Pallas kernels, per_device(): pl.pallas_call(kernel, out_shape=(pltpu.VMEM((1, TOK, HW), BF16),) * 2, i...  50.6 us

profile of v6, /device:TPU:6, one launch (start us, length us, event | category | flops | bytes accessed | tf_op | source)
XLA Modules:
  0.0 52.2 jit_solution(13794916581993632140)
XLA Ops:
  0.6 50.6 %shard_map.68 = (bf16[1,64,2560]{2,1,0:T(8,128)(2,1)S(1)}, bf16[1,64,2560]{2,1,0:T(8,128)(2,1)S(1)}) custom-call(bf16[1,64,2560]{2,1,0:T(8,128)(2,1)} %latent_hbm.1, bf16[2,16,2560]{2,1,0:T(8,128)(2,1)} %cache_hbm.1, s32[1,1,4]{2,1,0:T(1,128)} %mask_hbm.1, f32[2,2560]{1,0:T(2,128)} %gains_hbm.1, f32[2]{0:T(128)} %steps_hbm.1), custom_call_target="tpu_custom_call" | custom-call | flops 760000000 | bytes 1200000 | tf_op jit(solution)/shard_map/pallas_call | solution.py:530
  51.3 0.9 %shard_map.69 = (bf16[1,64,2560]{2,1,0:T(8,128)(2,1)}, bf16[1,64,2560]{2,1,0:T(8,128)(2,1)}) custom-call(bf16[1,64,2560]{2,1,0:T(8,128)(2,1)S(1)} %get-tuple-element.4.denoised_in, bf16[1,64,2560]{2,1,0:T(8,128)(2,1)S(1)} %get-tuple-element.5.velocity_in), custom_call_target="tpu_custom_call" | custom-call | tf_op jit(solution)/shard_map/pallas_call | solution.py:563

commit v7 on v6

--- a/solution.py
+++ b/solution.py
@@ -305,8 +305,6 @@
         pltpu.make_async_copy(gains_hbm, gains_ref, local_sem.at[4]),
         pltpu.make_async_copy(steps_hbm, steps_ref, local_sem.at[5]),
     ]
-    for load in loads:
-        load.start()
     barrier = pltpu.get_barrier_semaphore()
     for device in (*along_y, sibling):
         pl.semaphore_signal(barrier, inc=1, device_id=device, device_id_type=MESH)
@@ -315,13 +313,12 @@
         def _():
             pl.semaphore_signal(barrier, inc=1, device_id=along_z[direction], device_id_type=MESH)
 
+    for load in loads:
+        load.start()
     pl.semaphore_wait(barrier, 3 + lax.min(space, 1) + lax.min(n_space - 1 - space, 1))
 
-    for number in range(2):
-        for direction in range(2):
-            ring_copy(direction, number, True).start()
     start_tile(0, 0, 0)
-    for number in range(2, 4):
+    for number in range(4):
         for direction in range(2):
             ring_copy(direction, number, True).start()
     for which in range(2):
@@ -405,18 +402,13 @@
             update(phase, (every[2 * PER :], ((0, 3),)))
 
         near, far = ((NEAR, 1),), ((FAR, 1),)
-        for group in range(2):
+        for group in range(GROUPS):
             rounds(2 * group, 2)
             wait_tile(phase, 0, group)
-        take_scales(phase, 0)
-        update(phase, (every[: 2 * PER], near))
-        rounds(4, 2)
-        wait_tile(phase, 0, 2)
-        update(phase, (every[2 * PER : 3 * PER], near))
-        rounds(6, 2)
-        wait_tile(phase, 0, 3)
+            if group == 0:
+                take_scales(phase, 0)
+            update(phase, (every[group * PER : (group + 1) * PER], near))
         rounds(8, 2)
-        update(phase, (every[3 * PER :], near))
 
         @pl.when(first)
         def _():
@@ -440,11 +432,10 @@
         def _():
             last_shards(0)
             update(phase, (every[: 2 * PER], ((2, 1),)))
-            finish(every[: 2 * PER])
             last_shards(1)
             wait_tile(phase, 1, 3)
             update(phase, (every[2 * PER : 3 * PER], ((2, 1),)), (every[3 * PER :], ((2, 1), (FAR, 1))))
-            finish(every[2 * PER :])
+            finish(every)
 
         @pl.when(jnp.logical_not(first))
         def _():

time: 52.3 us -> 51.6 us (0.987)
  Pallas kernels: 51.5 us -> 50.8 us
    pallas_call x1, Pallas kernels: 50.6 us -> 49.9 us  [per_device(): pl.pallas_call(kernel, out_shape=(pltpu.VMEM((1, TOK, HW), BF16),) * 2, i...]
where the time goes in v7:
time: 51.6 us; the launch traced here: 51.5 us
  Pallas kernels  50.8 us (98%)
  between operations  0.64 us (1%)
    pallas_call x1, Pallas kernels, per_device(): pl.pallas_call(kernel, out_shape=(pltpu.VMEM((1, TOK, HW), BF16),) * 2, i...  49.9 us

profile of v7, /device:TPU:6, one launch (start us, length us, event | category | flops | bytes accessed | tf_op | source)
XLA Modules:
  0.0 51.5 jit_solution(17258313087793522382)
XLA Ops:
  0.6 49.9 %shard_map.68 = (bf16[1,64,2560]{2,1,0:T(8,128)(2,1)S(1)}, bf16[1,64,2560]{2,1,0:T(8,128)(2,1)S(1)}) custom-call(bf16[1,64,2560]{2,1,0:T(8,128)(2,1)} %latent_hbm.1, bf16[2,16,2560]{2,1,0:T(8,128)(2,1)} %cache_hbm.1, s32[1,1,4]{2,1,0:T(1,128)} %mask_hbm.1, f32[2,2560]{1,0:T(2,128)} %gains_hbm.1, f32[2]{0:T(128)} %steps_hbm.1), custom_call_target="tpu_custom_call" | custom-call | flops 760000000 | bytes 1200000 | tf_op jit(solution)/shard_map/pallas_call | solution.py:521
  50.6 0.9 %shard_map.69 = (bf16[1,64,2560]{2,1,0:T(8,128)(2,1)}, bf16[1,64,2560]{2,1,0:T(8,128)(2,1)}) custom-call(bf16[1,64,2560]{2,1,0:T(8,128)(2,1)S(1)} %get-tuple-element.4.denoised_in, bf16[1,64,2560]{2,1,0:T(8,128)(2,1)S(1)} %get-tuple-element.5.velocity_in), custom_call_target="tpu_custom_call" | custom-call | tf_op jit(solution)/shard_map/pallas_call | solution.py:554

commit v8 on v7

--- a/solution.py
+++ b/solution.py
@@ -210,55 +210,70 @@
         scales = scale_col[pl.ds((stage - NEAR) * STAGE, STAGE), :]
         return (buf[1, rows, cols].astype(F32) * scales * gains_ref[1:2, cols]).astype(BF16)
 
-    def mix(plan, weights, phase):
-        mixed = []
-        at = 0
-        while at < len(plan):
-            head, spans = plan[at]
-            pair = 2 if at + 1 < len(plan) and plan[at + 1] == (head + 1, spans) else 1
-            cols = pl.ds(head * HD, pair * HD)
-            sums = None
-            for i, (stage, count) in enumerate(spans):
-                stacked = jnp.concatenate([weights[at + j][i] for j in range(pair)], axis=0)
-                product = jnp.dot(stacked, buf[1, value_rows(stage, count, phase), cols], preferred_element_type=F32)
-                sums = product if sums is None else sums + product
-            mixed += [sums[j * TOK : (j + 1) * TOK, j * HD : (j + 1) * HD] for j in range(pair)]
-            at += pair
-        return mixed
-
     def update(phase, *parts):
         plan = [(head, spans) for heads, spans in parts for head in heads]
-        cols = [head_cols(head) for head, _ in plan]
-        keys = [[keys_of(head, stage, count, phase) for stage, count in spans] for head, spans in plan]
-        queries = [query[:, c] for c in cols]
-        old_peaks = [peak[head] for head, _ in plan]
-        scores = []
-        for q, each, (_, spans) in zip(queries, keys, plan):
-            pieces = []
-            for k, (stage, count) in zip(each, spans):
-                raw = lax.dot_general(q, k, (((1,), (1,)), ((), ())), preferred_element_type=F32)
-                pieces.append([
-                    raw[:, i * STAGE : (i + 1) * STAGE] * SCORE_SCALE + bias[stage + i, 0:1, :] for i in range(count)
-                ])
-            scores.append(pieces)
-        tops = [functools.reduce(jnp.maximum, sum(pieces, [])) for pieces in scores]
-        peaks = [
-            jnp.maximum(old, jnp.broadcast_to(jnp.max(top, axis=1, keepdims=True), (TOK, HD)))
-            for old, top in zip(old_peaks, tops)
-        ]
-        expos = [[[jnp.exp2(s - p) for s in span] for span in pieces] for pieces, p in zip(scores, peaks)]
-        weights = [[jnp.concatenate([e.astype(BF16) for e in span], axis=1) for span in each] for each in expos]
-        mixed = mix(plan, weights, phase)
-        factors = [jnp.exp2(old - new) for old, new in zip(old_peaks, peaks)]
-        totals = [
-            total[head] * f + functools.reduce(jnp.add, sum(each, []))
-            for (head, _), f, each in zip(plan, factors, expos)
-        ]
-        sums = [accum[:, c] * f + m for c, f, m in zip(cols, factors, mixed)]
-        for i, (head, _) in enumerate(plan):
-            peak[head] = peaks[i]
-            total[head] = totals[i]
-            accum[:, cols[i]] = sums[i]
+        units = []
+        while plan:
+            head, spans = plan[0]
+            pair = 2 if len(plan) > 1 and plan[1] == (head + 1, spans) else 1
+            units.append((range(head, head + pair), spans))
+            plan = plan[pair:]
+
+        def score(unit, held):
+            heads, spans = unit
+            held["scores"] = []
+            for head in heads:
+                q = query[:, head_cols(head)]
+                pieces = []
+                for stage, count in spans:
+                    k = keys_of(head, stage, count, phase)
+                    raw = lax.dot_general(q, k, (((1,), (1,)), ((), ())), preferred_element_type=F32)
+                    pieces.append([
+                        raw[:, i * STAGE : (i + 1) * STAGE] * SCORE_SCALE + bias[stage + i, 0:1, :]
+                        for i in range(count)
+                    ])
+                held["scores"].append(pieces)
+
+        def top(unit, held):
+            heads, _ = unit
+            held["old"] = [peak[head] for head in heads]
+            tops = [functools.reduce(jnp.maximum, sum(pieces, [])) for pieces in held["scores"]]
+            held["peaks"] = [
+                jnp.maximum(old, jnp.broadcast_to(jnp.max(t, axis=1, keepdims=True), (TOK, HD)))
+                for old, t in zip(held["old"], tops)
+            ]
+
+        def mix(unit, held):
+            heads, spans = unit
+            held["expos"] = [
+                [[jnp.exp2(s - p) for s in span] for span in pieces] for pieces, p in zip(held["scores"], held["peaks"])
+            ]
+            cols = pl.ds(heads[0] * HD, len(heads) * HD)
+            product = None
+            for i, (stage, count) in enumerate(spans):
+                weights = jnp.concatenate(
+                    [jnp.concatenate([e.astype(BF16) for e in each[i]], axis=1) for each in held["expos"]], axis=0
+                )
+                values = buf[1, value_rows(stage, count, phase), cols]
+                part = jnp.dot(weights, values, preferred_element_type=F32)
+                product = part if product is None else product + part
+            held["mixed"] = [product[j * TOK : (j + 1) * TOK, j * HD : (j + 1) * HD] for j in range(len(heads))]
+
+        def keep(unit, held):
+            for i, head in enumerate(unit[0]):
+                factor = jnp.exp2(held["old"][i] - held["peaks"][i])
+                added = functools.reduce(jnp.add, sum(held["expos"][i], []))
+                peak[head] = held["peaks"][i]
+                total[head] = total[head] * factor + added
+                accum[:, head_cols(head)] = accum[:, head_cols(head)] * factor + held["mixed"][i]
+            held.clear()
+
+        steps = (score, top, mix, keep)
+        held = [{} for _ in units]
+        for at in range(len(units) + len(steps) - 1):
+            for behind in reversed(range(len(steps))):
+                if 0 <= at - behind < len(units):
+                    steps[behind](units[at - behind], held[at - behind])
 
     def finish(heads):
         attended = [accum[:, head_cols(head)] / jnp.sum(total[head], axis=1, keepdims=True) for head in heads]

time: 51.6 us -> 52.5 us (1.017)
  Pallas kernels: 50.8 us -> 51.7 us
    pallas_call x1, Pallas kernels: 49.9 us -> 50.8 us  [per_device(): pl.pallas_call(kernel, out_shape=(pltpu.VMEM((1, TOK, HW), BF16),) * 2, i...]
where the time goes in v8:
time: 52.5 us; the launch traced here: 52.3 us
  Pallas kernels  51.7 us (98%)
  between operations  0.64 us (1%)
    pallas_call x1, Pallas kernels, per_device(): pl.pallas_call(kernel, out_shape=(pltpu.VMEM((1, TOK, HW), BF16),) * 2, i...  50.8 us

profile of v8, /device:TPU:6, one launch (start us, length us, event | category | flops | bytes accessed | tf_op | source)
XLA Modules:
  0.0 52.3 jit_solution(11190165601197985069)
XLA Ops:
  0.6 50.8 %shard_map.68 = (bf16[1,64,2560]{2,1,0:T(8,128)(2,1)S(1)}, bf16[1,64,2560]{2,1,0:T(8,128)(2,1)S(1)}) custom-call(bf16[1,64,2560]{2,1,0:T(8,128)(2,1)} %latent_hbm.1, bf16[2,16,2560]{2,1,0:T(8,128)(2,1)} %cache_hbm.1, s32[1,1,4]{2,1,0:T(1,128)} %mask_hbm.1, f32[2,2560]{1,0:T(2,128)} %gains_hbm.1, f32[2]{0:T(128)} %steps_hbm.1), custom_call_target="tpu_custom_call" | custom-call | flops 760000000 | bytes 1200000 | tf_op jit(solution)/shard_map/pallas_call | solution.py:536
  51.4 0.9 %shard_map.69 = (bf16[1,64,2560]{2,1,0:T(8,128)(2,1)}, bf16[1,64,2560]{2,1,0:T(8,128)(2,1)}) custom-call(bf16[1,64,2560]{2,1,0:T(8,128)(2,1)S(1)} %get-tuple-element.4.denoised_in, bf16[1,64,2560]{2,1,0:T(8,128)(2,1)S(1)} %get-tuple-element.5.velocity_in), custom_call_target="tpu_custom_call" | custom-call | tf_op jit(solution)/shard_map/pallas_call | solution.py:569

commit v9 on v7

--- a/solution.py
+++ b/solution.py
@@ -30,13 +30,14 @@
 ROWS = TILES + STEPS * 2 * STAGE
 CHIP = TOK
 RING = 14
+LAST = 15
 
 
 def kernel(
     latent_hbm, cache_hbm, mask_hbm, gains_hbm, steps_hbm,
     denoised_ref, velocity_ref,
     mask_ref, gains_ref, steps_ref, buf, query, accum, peak, total, scale_own, scale_in, scale_col, bias, square,
-    local_sem, ysend, ssend, yrecv, zsend, zrecv, rsend, rrecv,
+    local_sem, ysend, ssend, yrecv, srecv, zsend, zrecv, rsend, rrecv,
 ):
     tm, space = lax.axis_index("tm"), lax.axis_index("space")
     n_tm, n_space = lax.axis_size("tm"), lax.axis_size("space")
@@ -53,18 +54,19 @@
         )
 
     def half_cols(half):
-        return pl.ds(pl.multiple_of(half * (HW // 2), HW // 2), HW // 2)
-
-    def shard(which, index, half):
-        rows = CHIP + SHARD * index + jnp.where(index >= 2, 2 * SHARD, 0)
-        return buf.at[which, pl.ds(pl.multiple_of(rows, SHARD), SHARD), half_cols(half)]
+        return pl.ds(half * (HW // 2), HW // 2)
+
+    def shard(which, index, half=None):
+        rows = CHIP + SHARD * index + (2 * SHARD if index >= 2 else 0)
+        if half is None:
+            return buf.at[which, pl.ds(rows, SHARD)]
+        return buf.at[which, pl.ds(rows, SHARD), half_cols(half)]
 
     def slot(distance, direction):
-        return 4 * distance - 2 + jnp.where(distance == 4, 0, 2 * direction)
+        return 4 * distance - 2 + (0 if distance == 4 else 2 * direction)
 
     def ring_place(direction, number):
-        which = lax.rem(number // 2 + direction, 2)
-        return which, lax.rem(number, 2), number // 4 + 1
+        return (number // 2 + direction) % 2, number % 2, number // 4 + 1
 
     def ring_copy(direction, number, own):
         which, half, distance = ring_place(direction, number)
@@ -72,35 +74,40 @@
         if own:
             src = cache_hbm.at[which, :, half_cols(half)]
         else:
-            src = shard(which, slot(distance - 1, direction), half)
+            src = shard(which, slot(distance - 1, direction) if distance > 1 else 0, half)
         return remote(
             src, shard(which, target, half), ysend.at[direction, number], yrecv.at[which, target, half],
             along_y[direction],
         )
 
-    def sib_copy(which, half, target, own=False):
-        src = cache_hbm.at[which, :, half_cols(half)] if own else shard(which, target - 1, half)
-        return remote(
-            src, shard(which, target, half), ssend.at[which, target, half], yrecv.at[which, target, half], sibling
-        )
+    def sib_copy(which, target, half=None, own=False):
+        if own:
+            src, dst = cache_hbm.at[which], shard(which, target)
+        else:
+            src, dst = shard(which, target - 1, half), shard(which, target, half)
+        sem = 0 if half is None else half
+        return remote(src, dst, ssend.at[which, target, sem], srecv.at[which, target, sem], sibling)
 
     def ring_round(number):
         for direction in range(2):
+            ring_copy(direction, number, False).wait_recv()
+            if number + 4 < RING:
+                ring_copy(direction, number + 4, False).start()
+        for direction in range(2):
             which, half, distance = ring_place(direction, number)
-            ring_copy(direction, number, False).wait_recv()
-
-            @pl.when(number + 4 < RING)
-            def _():
-                ring_copy(direction, number + 4, False).start()
-
-            sib_copy(which, half, slot(distance, direction) + 1).start()
-
-    def each_sibling(first, count, act):
-        def body(i, _):
-            act(sib_copy(lax.rem(i, 2), lax.rem(i // 2, 2), first + 2 * (i // 4)))
-            return 0
-
-        lax.fori_loop(0, 4 * count, body, 0)
+            if distance == 4:
+                sib_copy(which, LAST, half).start()
+            elif half == 1:
+                sib_copy(which, slot(distance, direction) + 1).start()
+
+    def each_sibling(targets, act):
+        for target in targets:
+            for which in range(2):
+                if target == LAST:
+                    for half in range(2):
+                        act(sib_copy(which, target, half))
+                else:
+                    act(sib_copy(which, target))
 
     def columns(group):
         return pl.ds(pl.multiple_of(group * GW, GW), GW)
@@ -281,19 +288,10 @@
                 lax.fori_loop(0, GROUPS, body, 0)
 
     def earlier_sends_left():
-        def ring_left(number, _):
+        for number in range(RING):
             for direction in range(2):
-                ring_copy(direction, number, False).wait_send()
-            return 0
-
-        for number in range(4):
-            for direction in range(2):
-                ring_copy(direction, number, True).wait_send()
-        lax.fori_loop(4, RING, ring_left, 0)
-        for which in range(2):
-            for half in range(2):
-                sib_copy(which, half, 1, True).wait_send()
-        each_sibling(3, 7, lambda copy: copy.wait_send())
+                ring_copy(direction, number, number < 4).wait_send()
+        each_sibling(range(1, LAST + 1, 2), lambda copy: copy.wait_send())
         for hop in range(2):
             tiles_left(0, hop)
 
@@ -322,8 +320,7 @@
         for direction in range(2):
             ring_copy(direction, number, True).start()
     for which in range(2):
-        for half in range(2):
-            sib_copy(which, half, 1, True).start()
+        sib_copy(which, 1, own=True).start()
 
     for hop in range(2):
         for direction in range(2):
@@ -382,15 +379,16 @@
                     ring_round(number)
 
         def last_shards(half):
-            for target in (11, 13, 15):
-                for which in range(2):
-                    sib_copy(which, half, target).wait_recv()
+            if half == 0:
+                each_sibling((11, 13), lambda copy: copy.wait_recv())
+            for which in range(2):
+                sib_copy(which, LAST, half).wait_recv()
 
         every = range(HEADS)
 
         @pl.when(first)
         def _():
-            each_sibling(1, 1, lambda copy: copy.wait_recv())
+            each_sibling((1,), lambda copy: copy.wait_recv())
 
         @pl.when(first)
         def _():
@@ -412,7 +410,7 @@
 
         @pl.when(first)
         def _():
-            each_sibling(3, 4, lambda copy: copy.wait_recv())
+            each_sibling((3, 5, 7, 9), lambda copy: copy.wait_recv())
             update(phase, (every, ((1, 1),)))
 
         @pl.when(jnp.logical_not(first))
@@ -440,6 +438,7 @@
         @pl.when(jnp.logical_not(first))
         def _():
             finish(every[: 3 * PER])
+            tiles_left(1, 0)
             wait_tile(phase, 1, 3)
             update(phase, (every[3 * PER :], far))
             finish(every[3 * PER :])
@@ -490,8 +489,7 @@
         denoised_ref[0, :, c] = denoised.astype(BF16)
         velocity_ref[0, :, c] = velocity.astype(BF16)
 
-    for hop in range(2):
-        tiles_left(1, hop)
+    tiles_left(1, 1)
 
 
 PIECE = 16
@@ -541,6 +539,7 @@
             dma((2, RING)),
             dma((2, 16, 2)),
             dma((2, 16, 2)),
+            dma((2, 16, 2)),
             dma((STEPS, 2, 2, GROUPS)),
             dma((STEPS, 4, GROUPS)),
             dma((STEPS, 2, 2)),

time: 51.6 us -> 52.1 us (level)
  Pallas kernels: 50.8 us -> 51.4 us
where the time goes in v9:
time: 52.1 us; the launch traced here: 52 us
  Pallas kernels  51.4 us (99%)
  between operations  0.64 us (1%)
    pallas_call x1, Pallas kernels, per_device(): pl.pallas_call(kernel, out_shape=(pltpu.VMEM((1, TOK, HW), BF16),) * 2, i...  50.5 us

profile of v9, /device:TPU:6, one launch (start us, length us, event | category | flops | bytes accessed | tf_op | source)
XLA Modules:
  0.0 52.0 jit_solution(6890316111173040618)
XLA Ops:
  0.6 50.5 %shard_map.68 = (bf16[1,64,2560]{2,1,0:T(8,128)(2,1)S(1)}, bf16[1,64,2560]{2,1,0:T(8,128)(2,1)S(1)}) custom-call(bf16[1,64,2560]{2,1,0:T(8,128)(2,1)} %latent_hbm.1, bf16[2,16,2560]{2,1,0:T(8,128)(2,1)} %cache_hbm.1, s32[1,1,4]{2,1,0:T(1,128)} %mask_hbm.1, f32[2,2560]{1,0:T(2,128)} %gains_hbm.1, f32[2]{0:T(128)} %steps_hbm.1), custom_call_target="tpu_custom_call" | custom-call | flops 760000000 | bytes 1200000 | tf_op jit(solution)/shard_map/pallas_call | solution.py:519
  51.1 0.9 %shard_map.69 = (bf16[1,64,2560]{2,1,0:T(8,128)(2,1)}, bf16[1,64,2560]{2,1,0:T(8,128)(2,1)}) custom-call(bf16[1,64,2560]{2,1,0:T(8,128)(2,1)S(1)} %get-tuple-element.4.denoised_in, bf16[1,64,2560]{2,1,0:T(8,128)(2,1)S(1)} %get-tuple-element.5.velocity_in), custom_call_target="tpu_custom_call" | custom-call | tf_op jit(solution)/shard_map/pallas_call | solution.py:553

commit v10 on v7

--- a/solution.py
+++ b/solution.py
@@ -260,6 +260,33 @@
             total[head] = totals[i]
             accum[:, cols[i]] = sums[i]
 
+    def tile_update(phase, hop, group):
+        heads = [group * PER + i for i in range(PER)]
+        cols = [head_cols(head) for head in heads]
+        rows = pl.ds(pl.multiple_of((NEAR + hop + phase * 2) * STAGE, STAGE), STAGE)
+        scales = scale_col[pl.ds(pl.multiple_of(hop * STAGE, STAGE), STAGE), :]
+        allowed = bias[NEAR + hop, 0:1, :]
+        old_peaks = [peak[head] for head in heads]
+        values = [buf[1, rows, c] for c in cols]
+        keys = [(v.astype(F32) * scales * gains_ref[1:2, c]).astype(BF16) for v, c in zip(values, cols)]
+        scores = [
+            lax.dot_general(query[:, c], k, (((1,), (1,)), ((), ())), preferred_element_type=F32) * SCORE_SCALE + allowed
+            for c, k in zip(cols, keys)
+        ]
+        peaks = [
+            jnp.maximum(old, jnp.broadcast_to(jnp.max(s, axis=1, keepdims=True), (TOK, HD)))
+            for old, s in zip(old_peaks, scores)
+        ]
+        expos = [jnp.exp2(s - p) for s, p in zip(scores, peaks)]
+        mixed = [jnp.dot(e.astype(BF16), v, preferred_element_type=F32) for e, v in zip(expos, values)]
+        factors = [jnp.exp2(old - new) for old, new in zip(old_peaks, peaks)]
+        totals = [total[head] * f + e for head, f, e in zip(heads, factors, expos)]
+        sums = [accum[:, c] * f + m for c, f, m in zip(cols, factors, mixed)]
+        for i, head in enumerate(heads):
+            peak[head] = peaks[i]
+            total[head] = totals[i]
+            accum[:, cols[i]] = sums[i]
+
     def finish(heads):
         attended = [accum[:, head_cols(head)] / jnp.sum(total[head], axis=1, keepdims=True) for head in heads]
         squares = square[...]
@@ -401,48 +428,55 @@
             update(phase, (every[: 2 * PER], ((0, 3),)))
             update(phase, (every[2 * PER :], ((0, 3),)))
 
-        near, far = ((NEAR, 1),), ((FAR, 1),)
-        for group in range(GROUPS):
-            rounds(2 * group, 2)
-            wait_tile(phase, 0, group)
-            if group == 0:
+        def tile_part_step(number, _):
+            hop, group = number // GROUPS, lax.rem(number, GROUPS)
+
+            @pl.when(first & (number < 7))
+            def _():
+                ring_round(2 * number)
+                ring_round(2 * number + 1)
+
+            @pl.when(first & (number == GROUPS))
+            def _():
+                each_sibling(3, 4, lambda copy: copy.wait_recv())
+                update(phase, (every, ((1, 1),)))
+
+            @pl.when(jnp.logical_not(first) & (number == GROUPS))
+            def _():
+                earlier_sends_left()
+
+            @pl.when(number == 2 * GROUPS - 1)
+            def _():
+                @pl.when(first)
+                def _():
+                    last_shards(0)
+                    update(phase, (every[: 2 * PER], ((2, 1),)))
+                    last_shards(1)
+                    update(phase, (every[2 * PER :], ((2, 1),)))
+
+                finish(every[: 3 * PER])
+
+            @pl.when(hop == 0)
+            def _():
+                wait_tile(phase, 0, group)
+
+            @pl.when(hop == 1)
+            def _():
+                wait_tile(phase, 1, group)
+
+            @pl.when(number == 0)
+            def _():
                 take_scales(phase, 0)
-            update(phase, (every[group * PER : (group + 1) * PER], near))
-        rounds(8, 2)
-
-        @pl.when(first)
-        def _():
-            each_sibling(3, 4, lambda copy: copy.wait_recv())
-            update(phase, (every, ((1, 1),)))
-
-        @pl.when(jnp.logical_not(first))
-        def _():
-            earlier_sends_left()
-
-        rounds(10, 2)
-        wait_tile(phase, 1, 0)
-        wait_tile(phase, 1, 1)
-        take_scales(phase, 1)
-        update(phase, (every[: 2 * PER], far))
-        rounds(12, 2)
-        wait_tile(phase, 1, 2)
-        update(phase, (every[2 * PER : 3 * PER], far))
-
-        @pl.when(first)
-        def _():
-            last_shards(0)
-            update(phase, (every[: 2 * PER], ((2, 1),)))
-            last_shards(1)
-            wait_tile(phase, 1, 3)
-            update(phase, (every[2 * PER : 3 * PER], ((2, 1),)), (every[3 * PER :], ((2, 1), (FAR, 1))))
-            finish(every)
-
-        @pl.when(jnp.logical_not(first))
-        def _():
-            finish(every[: 3 * PER])
-            wait_tile(phase, 1, 3)
-            update(phase, (every[3 * PER :], far))
-            finish(every[3 * PER :])
+
+            @pl.when(number == GROUPS)
+            def _():
+                take_scales(phase, 1)
+
+            tile_update(phase, hop, group)
+            return 0
+
+        lax.fori_loop(0, 2 * GROUPS, tile_part_step, 0)
+        finish(every[3 * PER :])
 
         @pl.when(first)
         def _():

time: 51.6 us -> 52.4 us (1.016)
  Pallas kernels: 50.8 us -> 51.6 us
    pallas_call x1, Pallas kernels: 49.9 us -> 50.7 us  [per_device(): pl.pallas_call(kernel, out_shape=(pltpu.VMEM((1, TOK, HW), BF16),) * 2, i...]
where the time goes in v10:
time: 52.4 us; the launch traced here: 52.3 us
  Pallas kernels  51.6 us (98%)
  between operations  0.64 us (1%)
    pallas_call x1, Pallas kernels, per_device(): pl.pallas_call(kernel, out_shape=(pltpu.VMEM((1, TOK, HW), BF16),) * 2, i...  50.7 us

profile of v10, /device:TPU:6, one launch (start us, length us, event | category | flops | bytes accessed | tf_op | source)
XLA Modules:
  0.0 52.3 jit_solution(10297283286952235626)
XLA Ops:
  0.6 50.7 %shard_map.68 = (bf16[1,64,2560]{2,1,0:T(8,128)(2,1)S(1)}, bf16[1,64,2560]{2,1,0:T(8,128)(2,1)S(1)}) custom-call(bf16[1,64,2560]{2,1,0:T(8,128)(2,1)} %latent_hbm.1, bf16[2,16,2560]{2,1,0:T(8,128)(2,1)} %cache_hbm.1, s32[1,1,4]{2,1,0:T(1,128)} %mask_hbm.1, f32[2,2560]{1,0:T(2,128)} %gains_hbm.1, f32[2]{0:T(128)} %steps_hbm.1), custom_call_target="tpu_custom_call" | custom-call | flops 760000000 | bytes 1200000 | tf_op jit(solution)/shard_map/pallas_call | solution.py:555
  51.4 0.9 %shard_map.69 = (bf16[1,64,2560]{2,1,0:T(8,128)(2,1)}, bf16[1,64,2560]{2,1,0:T(8,128)(2,1)}) custom-call(bf16[1,64,2560]{2,1,0:T(8,128)(2,1)S(1)} %get-tuple-element.4.denoised_in, bf16[1,64,2560]{2,1,0:T(8,128)(2,1)S(1)} %get-tuple-element.5.velocity_in), custom_call_target="tpu_custom_call" | custom-call | tf_op jit(solution)/shard_map/pallas_call | solution.py:588

commit v11 on v7

--- a/solution.py
+++ b/solution.py
@@ -14,7 +14,7 @@
 TOK = 64
 STEPS = 2
 SHARD = 16
-GROUPS = 4
+GROUPS = 5
 PER = HEADS // GROUPS
 GW = PER * HD
 EPS = 1e-6
@@ -398,8 +398,8 @@
 
         @pl.when(jnp.logical_not(first))
         def _():
-            update(phase, (every[: 2 * PER], ((0, 3),)))
-            update(phase, (every[2 * PER :], ((0, 3),)))
+            update(phase, (every[: HEADS // 2], ((0, 3),)))
+            update(phase, (every[HEADS // 2 :], ((0, 3),)))
 
         near, far = ((NEAR, 1),), ((FAR, 1),)
         for group in range(GROUPS):
@@ -408,7 +408,6 @@
             if group == 0:
                 take_scales(phase, 0)
             update(phase, (every[group * PER : (group + 1) * PER], near))
-        rounds(8, 2)
 
         @pl.when(first)
         def _():
@@ -426,23 +425,24 @@
         update(phase, (every[: 2 * PER], far))
         rounds(12, 2)
         wait_tile(phase, 1, 2)
-        update(phase, (every[2 * PER : 3 * PER], far))
+        wait_tile(phase, 1, 3)
+        update(phase, (every[2 * PER : 4 * PER], far))
 
         @pl.when(first)
         def _():
             last_shards(0)
-            update(phase, (every[: 2 * PER], ((2, 1),)))
+            update(phase, (every[: HEADS // 2], ((2, 1),)))
             last_shards(1)
-            wait_tile(phase, 1, 3)
-            update(phase, (every[2 * PER : 3 * PER], ((2, 1),)), (every[3 * PER :], ((2, 1), (FAR, 1))))
+            wait_tile(phase, 1, 4)
+            update(phase, (every[HEADS // 2 : 4 * PER], ((2, 1),)), (every[4 * PER :], ((2, 1), (FAR, 1))))
             finish(every)
 
         @pl.when(jnp.logical_not(first))
         def _():
-            finish(every[: 3 * PER])
-            wait_tile(phase, 1, 3)
-            update(phase, (every[3 * PER :], far))
-            finish(every[3 * PER :])
+            finish(every[: 4 * PER])
+            wait_tile(phase, 1, 4)
+            update(phase, (every[4 * PER :], far))
+            finish(every[4 * PER :])
 
         @pl.when(first)
         def _():

time: 51.6 us -> 51.6 us (level)
  no operation moved by 1% of the time
where the time goes in v11:
time: 51.6 us; the launch traced here: 51.5 us
  Pallas kernels  50.9 us (99%)
  between operations  0.64 us (1%)
    pallas_call x1, Pallas kernels, per_device(): pl.pallas_call(kernel, out_shape=(pltpu.VMEM((1, TOK, HW), BF16),) * 2, i...  50 us

profile of v11, /device:TPU:6, one launch (start us, length us, event | category | flops | bytes accessed | tf_op | source)
XLA Modules:
  0.0 51.5 jit_solution(1786051427699251199)
XLA Ops:
  0.6 50.0 %shard_map.68 = (bf16[1,64,2560]{2,1,0:T(8,128)(2,1)S(1)}, bf16[1,64,2560]{2,1,0:T(8,128)(2,1)S(1)}) custom-call(bf16[1,64,2560]{2,1,0:T(8,128)(2,1)} %latent_hbm.1, bf16[2,16,2560]{2,1,0:T(8,128)(2,1)} %cache_hbm.1, s32[1,1,4]{2,1,0:T(1,128)} %mask_hbm.1, f32[2,2560]{1,0:T(2,128)} %gains_hbm.1, f32[2]{0:T(128)} %steps_hbm.1), custom_call_target="tpu_custom_call" | custom-call | flops 760000000 | bytes 1200000 | tf_op jit(solution)/shard_map/pallas_call | solution.py:521
  50.6 0.9 %shard_map.69 = (bf16[1,64,2560]{2,1,0:T(8,128)(2,1)}, bf16[1,64,2560]{2,1,0:T(8,128)(2,1)}) custom-call(bf16[1,64,2560]{2,1,0:T(8,128)(2,1)S(1)} %get-tuple-element.4.denoised_in, bf16[1,64,2560]{2,1,0:T(8,128)(2,1)S(1)} %get-tuple-element.5.velocity_in), custom_call_target="tpu_custom_call" | custom-call | tf_op jit(solution)/shard_map/pallas_call | solution.py:554

commit v12 on v11

--- a/solution.py
+++ b/solution.py
@@ -317,10 +317,11 @@
         load.start()
     pl.semaphore_wait(barrier, 3 + lax.min(space, 1) + lax.min(n_space - 1 - space, 1))
 
-    start_tile(0, 0, 0)
-    for number in range(4):
-        for direction in range(2):
-            ring_copy(direction, number, True).start()
+    for part in range(2):
+        start_tile(0, 0, part)
+        for number in range(2 * part, 2 * part + 2):
+            for direction in range(2):
+                ring_copy(direction, number, True).start()
     for which in range(2):
         for half in range(2):
             sib_copy(which, half, 1, True).start()
@@ -365,7 +366,7 @@
     lax.fori_loop(0, GROUPS, add_squares, 0)
     col = root_scale()
     send_scale(0, col)
-    for group in range(1, GROUPS):
+    for group in range(2, GROUPS):
         start_tile(0, 0, group)
     begin_heads(col)
     for load in loads[1:3]:
@@ -405,9 +406,11 @@
         for group in range(GROUPS):
             rounds(2 * group, 2)
             wait_tile(phase, 0, group)
-            if group == 0:
+            if group == 1:
                 take_scales(phase, 0)
-            update(phase, (every[group * PER : (group + 1) * PER], near))
+                update(phase, (every[: 2 * PER], near))
+            elif group > 1:
+                update(phase, (every[group * PER : (group + 1) * PER], near))
 
         @pl.when(first)
         def _():

time: 51.6 us -> 51.6 us (level)
  no operation moved by 1% of the time
where the time goes in v12:
time: 51.6 us; the launch traced here: 51.5 us
  Pallas kernels  50.8 us (98%)
  between operations  0.64 us (1%)
    pallas_call x1, Pallas kernels, per_device(): pl.pallas_call(kernel, out_shape=(pltpu.VMEM((1, TOK, HW), BF16),) * 2, i...  49.9 us

profile of v12, /device:TPU:6, one launch (start us, length us, event | category | flops | bytes accessed | tf_op | source)
XLA Modules:
  0.0 51.5 jit_solution(664165217252721675)
XLA Ops:
  0.6 49.9 %shard_map.68 = (bf16[1,64,2560]{2,1,0:T(8,128)(2,1)S(1)}, bf16[1,64,2560]{2,1,0:T(8,128)(2,1)S(1)}) custom-call(bf16[1,64,2560]{2,1,0:T(8,128)(2,1)} %latent_hbm.1, bf16[2,16,2560]{2,1,0:T(8,128)(2,1)} %cache_hbm.1, s32[1,1,4]{2,1,0:T(1,128)} %mask_hbm.1, f32[2,2560]{1,0:T(2,128)} %gains_hbm.1, f32[2]{0:T(128)} %steps_hbm.1), custom_call_target="tpu_custom_call" | custom-call | flops 760000000 | bytes 1200000 | tf_op jit(solution)/shard_map/pallas_call | solution.py:524
  50.6 0.9 %shard_map.69 = (bf16[1,64,2560]{2,1,0:T(8,128)(2,1)}, bf16[1,64,2560]{2,1,0:T(8,128)(2,1)}) custom-call(bf16[1,64,2560]{2,1,0:T(8,128)(2,1)S(1)} %get-tuple-element.4.denoised_in, bf16[1,64,2560]{2,1,0:T(8,128)(2,1)S(1)} %get-tuple-element.5.velocity_in), custom_call_target="tpu_custom_call" | custom-call | tf_op jit(solution)/shard_map/pallas_call | solution.py:557

commit v13 on v11

--- a/solution.py
+++ b/solution.py
@@ -440,6 +440,7 @@
         @pl.when(jnp.logical_not(first))
         def _():
             finish(every[: 4 * PER])
+            tiles_left(1, 0)
             wait_tile(phase, 1, 4)
             update(phase, (every[4 * PER :], far))
             finish(every[4 * PER :])
@@ -490,11 +491,10 @@
         denoised_ref[0, :, c] = denoised.astype(BF16)
         velocity_ref[0, :, c] = velocity.astype(BF16)
 
-    for hop in range(2):
-        tiles_left(1, hop)
-
-
-PIECE = 16
+    tiles_left(1, 1)
+
+
+PIECE = 32
 PIECES = TOK // PIECE
 
 

time: 51.6 us -> 51.5 us (level)
  no operation moved by 1% of the time
where the time goes in v13:
time: 51.5 us; the launch traced here: 51.4 us
  Pallas kernels  50.8 us (99%)
  between operations  0.64 us (1%)
    pallas_call x1, Pallas kernels, per_device(): pl.pallas_call(kernel, out_shape=(pltpu.VMEM((1, TOK, HW), BF16),) * 2, i...  49.9 us

profile of v13, /device:TPU:6, one launch (start us, length us, event | category | flops | bytes accessed | tf_op | source)
XLA Modules:
  0.0 51.4 jit_solution(14437670578792064277)
XLA Ops:
  0.6 49.9 %shard_map.68 = (bf16[1,64,2560]{2,1,0:T(8,128)(2,1)S(1)}, bf16[1,64,2560]{2,1,0:T(8,128)(2,1)S(1)}) custom-call(bf16[1,64,2560]{2,1,0:T(8,128)(2,1)} %latent_hbm.1, bf16[2,16,2560]{2,1,0:T(8,128)(2,1)} %cache_hbm.1, s32[1,1,4]{2,1,0:T(1,128)} %mask_hbm.1, f32[2,2560]{1,0:T(2,128)} %gains_hbm.1, f32[2]{0:T(128)} %steps_hbm.1), custom_call_target="tpu_custom_call" | custom-call | flops 760000000 | bytes 1200000 | tf_op jit(solution)/shard_map/pallas_call | solution.py:521
  50.5 0.9 %shard_map.69 = (bf16[1,64,2560]{2,1,0:T(8,128)(2,1)}, bf16[1,64,2560]{2,1,0:T(8,128)(2,1)}) custom-call(bf16[1,64,2560]{2,1,0:T(8,128)(2,1)S(1)} %get-tuple-element.4.denoised_in, bf16[1,64,2560]{2,1,0:T(8,128)(2,1)S(1)} %get-tuple-element.5.velocity_in), custom_call_target="tpu_custom_call" | custom-call | tf_op jit(solution)/shard_map/pallas_call | solution.py:554
